TPU v7x, 256 devices: a whole 4x4x8 slice. The times are simulated.
256 devices in a mesh: wave: 16 (over x, y), lev: 16 (over z, core).
Axes of the slice: x: 4, y: 4, z: 8, core: 2. Of those that a mesh axis runs over, the one named last changes fastest.
Arguments:
- spectral: bfloat16 [6, 128, 1296, 640], P(None, 'lev', 'wave'), may hold values from -0.119628906 to 0.119628906
- legendre: bfloat16 [640, 1296, 32], P('wave'), may hold values from -0.15625 to 0.15625
- pair_list: int32 [640], replicated, may hold values from 0 to 639, each once
- lon_counts: int32 [32], replicated, may hold values from 20 to 5136, as said below
- lat_order: int32 [32], replicated, may hold values from 0 to 31, each once
- layer_depth_log: float32 [128], P('lev'), may hold values from 0.04 to 0.2
- diagonal_layer_factor: float32 [128], P('lev'), may hold values from 0.02 to 0.12
Outputs:
- vorticity_grid: float32 [32, 128, 5376], P('wave', 'lev')
- divergence_grid: float32 [32, 128, 5376], P('wave', 'lev')
- temperature_grid: float32 [32, 128, 5376], P('wave', 'lev')
- temperature_slope: float32 [32, 128, 5376], P('wave', 'lev')
- height_energy: float32 [32, 128, 5376], P('wave', 'lev')
Inputs may be any that keep to these rules, and one draw needn't show every extreme that they name: `pair_list`: a permutation; storage column s of spectral and legendre holds the wavenumbers pair_list[s] and 1279 - pair_list[s]. `lon_counts`: each value is 20 + 4 j for distinct j from 0 to 1279; the largest circle is always in the window. `lat_order`: A permutation.
All inputs are finite; a program needn't handle non-finite values.
Results may differ from a plain program's by a relative error of at most 0.0003.
Values may be sent and summed in bfloat16 or wider, within the bound.
A program may use at most 192 MiB of HBM per device.

v0:
```python
import jax
import jax.numpy as jnp
from jax import lax
from jax.sharding import PartitionSpec as P

TRUNC = 1279
ROWS = 1281
LON_PAD = 5376


def entering(value, axis, join, neutral):
    count, mine = (lax.axis_size(axis), lax.axis_index(axis))
    pieces = lax.all_gather(value, axis)
    pieces = pieces[::-1]
    mine = count - 1 - mine
    so_far = jnp.full_like(value, 0) + jnp.asarray(neutral, value.dtype)

    def lap(position, so_far):
        longer = join(so_far, pieces[position])
        return jnp.where(position < mine, longer, so_far)

    return lax.fori_loop(0, count - 1, lap, so_far)


def legendre_split(spec_rows, polynomials, pair_ids):
    row_index = lax.broadcasted_iota(jnp.int32, (spec_rows.shape[2], spec_rows.shape[3]), 0)
    boundary = TRUNC + 1 - pair_ids[None, :]
    low_mask = row_index < boundary
    high_mask = (row_index >= boundary) & (row_index < ROWS)
    zero_value = jnp.zeros((), spec_rows.dtype)
    first_part = jnp.where(low_mask, spec_rows, zero_value)
    second_part = jnp.where(high_mask, spec_rows, zero_value)
    stacked = jnp.stack([first_part, second_part], 0)
    return jnp.einsum("hclrp,prq->qhclp", stacked, polynomials, preferred_element_type=jnp.float32)


def synthesis_basis(wavenumbers, lon_totals, first_column, block_width):
    columns = first_column + lax.broadcasted_iota(jnp.int32, (1, 1, block_width), 2)
    wave_grid = wavenumbers[None, :, None]
    circle = lon_totals[:, None, None]
    phases = wave_grid * columns % circle
    angles = phases.astype(jnp.float32) / circle.astype(jnp.float32) * (2.0 * jnp.pi)
    kept_mask = (2 * wave_grid < circle) & (columns < circle)
    weights = jnp.where(kept_mask, jnp.where(wave_grid == 0, 1.0, 2.0), 0.0).astype(jnp.float32)
    return jnp.concatenate([weights * jnp.cos(angles), weights * jnp.sin(angles)], axis=1)


def synthesis_rows(harmonic_amplitude, wavenumbers):
    factors = wavenumbers.astype(jnp.float32) / (TRUNC + 1)
    rotation_rate_values = jnp.concatenate(
        [harmonic_amplitude[..., 0, :, :], -harmonic_amplitude[..., 1, :, :]], -1
    )
    spreading_rate_values = jnp.concatenate(
        [harmonic_amplitude[..., 2, :, :], -harmonic_amplitude[..., 3, :, :]], -1
    )
    thermal_state_values = jnp.concatenate(
        [harmonic_amplitude[..., 4, :, :], -harmonic_amplitude[..., 5, :, :]], -1
    )
    zonal_slope_values = jnp.concatenate(
        [-factors * harmonic_amplitude[..., 5, :, :], -factors * harmonic_amplitude[..., 4, :, :]],
        -1,
    )
    return jnp.stack(
        [rotation_rate_values, spreading_rate_values, thermal_state_values, zonal_slope_values], -3
    )


def synthesize(fourier, wavenumbers, own_counts):
    lat_share, _, _, level_count, pair_count = fourier.shape
    harmonic_amplitude = jnp.transpose(fourier, (0, 2, 3, 1, 4)).reshape(
        lat_share, 6, level_count, 2 * pair_count
    )
    left_rows = synthesis_rows(harmonic_amplitude, wavenumbers).reshape(
        lat_share, 4 * level_count, 4 * pair_count
    )
    zero_index = jnp.zeros((), jnp.int32)
    grid_empty = jnp.zeros((lat_share, 4 * level_count, LON_PAD), jnp.float32)

    def dense_block(block_number, grid_acc):
        first_column = block_number * 768
        basis_block = synthesis_basis(wavenumbers, own_counts, first_column, 768)
        product = jnp.einsum(
            "lrk,lkw->lrw",
            left_rows,
            basis_block,
            precision=lax.Precision.HIGHEST,
            preferred_element_type=jnp.float32,
        )
        return lax.dynamic_update_slice(grid_acc, product, (zero_index, zero_index, first_column))

    grid_full = lax.fori_loop(0, LON_PAD // 768, dense_block, grid_empty)
    return grid_full.reshape(lat_share, 4, level_count, LON_PAD)


def add_totals(earlier, later):
    return earlier + later


def body(
    spectral, legendre, pair_list, lon_counts, lat_order, layer_depth_log, diagonal_layer_factor
):
    group_count = lax.axis_size("wave")
    group_index = lax.axis_index("wave")
    pair_share = pair_list.shape[0] // group_count
    lat_share = lat_order.shape[0] // group_count
    own_pairs = lax.dynamic_slice_in_dim(pair_list, group_index * pair_share, pair_share)
    own_lats = lax.dynamic_slice_in_dim(lat_order, group_index * lat_share, lat_share)
    own_counts = jnp.take(lon_counts, own_lats)
    wavenumbers = jnp.concatenate([pair_list, TRUNC - pair_list])
    values = legendre_split(
        lax.all_to_all(spectral, "wave", split_axis=3, concat_axis=2, tiled=True),
        legendre,
        own_pairs,
    )
    fourier_slots = jnp.take(values, lat_order, axis=0)
    physical_space_lines = synthesize(
        lax.all_to_all(fourier_slots, "wave", split_axis=0, concat_axis=4, tiled=True),
        wavenumbers,
        own_counts,
    )
    thermal_state_values = physical_space_lines[:, 2]
    scaled_contributions = layer_depth_log[None, :, None] * thermal_state_values
    beneath_layers_total = (
        jnp.flip(jnp.cumsum(jnp.flip(scaled_contributions, 1), 1), 1) - scaled_contributions
    )
    column_total = jnp.sum(scaled_contributions, axis=1)
    carried_running = entering(column_total, "lev", add_totals, jnp.zeros_like(column_total))
    height_energy = (
        diagonal_layer_factor[None, :, None] * thermal_state_values
        + beneath_layers_total
        + carried_running[:, None, :]
    )
    return (
        physical_space_lines[:, 0],
        physical_space_lines[:, 1],
        thermal_state_values,
        physical_space_lines[:, 3],
        height_energy,
    )


def solution(mesh):
    placed = (
        P(None, "lev", "wave", None),
        P("wave", None, None),
        P(),
        P(),
        P(),
        P("lev"),
        P("lev"),
    )
    return jax.shard_map(
        body,
        mesh=mesh,
        in_specs=placed,
        out_specs=(
            P("wave", "lev", None),
            P("wave", "lev", None),
            P("wave", "lev", None),
            P("wave", "lev", None),
            P("wave", "lev", None),
        ),
        check_vma=False,
    )
```

profile of v0, /device:TPU:1, one launch (start us, length us, event | category | flops | bytes accessed | tf_op | source)
XLA Modules:
  0.0 1113.8 jit_solution(12333207180562067627)
XLA Ops:
  0.6 10.5 copy.44
  11.1 7.8 all-to-all-start
  19.0 0.6 compare_select_fusion.3
  19.6 0.5 compare_and_fusion
  20.3 134.1 %all-to-all-done = bf16[6,8,81,640]{2,1,0,3:T(8,128)(2,1)} async-done(((bf16[6,8,81,640]{2,1,0,3:T(8,128)(2,1)}), bf16[6,8,81,640]{2,1,0,3:T(8,128)(2,1)}, u32[]{:S(2)}, u32[]{:S(2)}) %all-to-all-start) | async-done | bytes 4976672 | tf_op jit(solution)/shard_map/all_to_all | solution.py:111
  154.4 15.5 %copy.46 = bf16[6,8,16,81,40]{3,2,1,0,4:T(8,128)(2,1)} copy(bf16[6,8,16,81,40]{3,1,0,4,2:T(8,128)(2,1)} %bitcast.5) | data formatting | bytes 9953280 | tf_op jit(solution)/shard_map/all_to_all | solution.py:111
  169.9 14.0 %all_to_all.29 = bf16[1,6,8,1296,40]{3,2,1,0,4:T(8,128)(2,1)} reshape(bf16[6,8,16,81,40]{3,2,1,0,4:T(8,128)(2,1)} %copy.46) | data formatting | bytes 9953280 | tf_op jit(solution)/shard_map/all_to_all | solution.py:111
  183.8 8.2 broadcast_select_fusion.1
  192.0 6.9 fusion.21
  199.0 1.4 copy.47
  200.3 0.7 gather_fusion.1
  201.0 0.8 broadcast_select_fusion.2
  201.8 2.3 reshape.245
  204.2 8.5 all-to-all-start.1
  212.7 0.6 gather_fusion
  213.5 8.0 all-to-all-done.1
  221.5 0.5 broadcast.266
  222.0 1.8 reduce
  223.8 1.3 reshape.246
  225.1 0.9 copy.48
  226.0 0.8 all_to_all.33
  227.2 855.7 %while.28 = (s32[]{:T(128)}, f32[2,32,5376]{2,1,0:T(8,128)S(1)}, s32[1280]{0:T(1024)S(1)}, s32[2]{0:T(128)S(1)}, f32[2,1,1]{0,2,1:T(1,128)S(1)}, /*index=5*/f32[...) while((s32[]{:T(128)}, f32[2,32,5376]{2,1,0:T(8,128)S(1)}, s32[1280]{0:T(1024)S(1)}, ...), condition=%wide.region_1.2_spmd, body=%wide.region_0.1_spmd.sunk | while | flops 1542398464 | bytes 40227032 | solution.py:91
  240.9 0.3 broadcast_multiply_fusion.6
  241.3 106.8 %select_multiply_fusion.3 = (f32[2,1280,768]{2,1,0:T(8,128)}, f32[2,1280,768]{2,1,0:T(8,128)}) fusion(f32[1280]{0:T(1024)S(1)} %compare_select_fusion.6, f32[2]{0:T(128)S(1)} %bitcast.107, pred[2]{0:T(512)(128)(4,1)S(1)} %broadcast_compare_fusion.6, s32[2]{0:T(128)S(1)} %compare_select_fusion.7, s32[1280,768]{1,0:T(8,128)S(1)} %broadcast_multiply_fusion.6, ...), kind=kLoop, calls=%fused_computation.11.clone.1 | loop fusion | flops 27525120 | bytes 19670034 | tf_op jit(solution)/shard_map/while/body/eval_jaxpr/mul | solution.py:45
  348.2 12.9 %fusion.41 = f32[2,32,5376]{2,1,0:T(8,128)S(1)} fusion(f32[2,32,5376]{2,1,0:T(8,128)S(1)} %get-tuple-element.342, s32[]{:T(128)S(6)} %select_n.180, f32[2,32,2560]{2,1,0:T(8,128)S(1)} %get-tuple-element.356, f32[2,1280,768]{2,1,0:T(8,128)} %get-tuple-element.325, f32[2,1280,768]{2,1,0:T(8,128)} %get-tuple-element.326), kind=kOutput, calls=%fused_computation.19.clone.1 | convolution fusion | flops 1513881600 | bytes 16580612 | tf_op jit(solution)/shard_map/while/body/eval_jaxpr/lrk,lkw->lrw/dot_general | solution.py:82
  361.2 0.3 broadcast_multiply_fusion.6
  361.6 106.8 %select_multiply_fusion.3 = (f32[2,1280,768]{2,1,0:T(8,128)}, f32[2,1280,768]{2,1,0:T(8,128)}) fusion(f32[1280]{0:T(1024)S(1)} %compare_select_fusion.6, f32[2]{0:T(128)S(1)} %bitcast.107, pred[2]{0:T(512)(128)(4,1)S(1)} %broadcast_compare_fusion.6, s32[2]{0:T(128)S(1)} %compare_select_fusion.7, s32[1280,768]{1,0:T(8,128)S(1)} %broadcast_multiply_fusion.6, ...), kind=kLoop, calls=%fused_computation.11.clone.1 | loop fusion | flops 27525120 | bytes 19670034 | tf_op jit(solution)/shard_map/while/body/eval_jaxpr/mul | solution.py:45
  468.5 12.9 %fusion.41 = f32[2,32,5376]{2,1,0:T(8,128)S(1)} fusion(f32[2,32,5376]{2,1,0:T(8,128)S(1)} %get-tuple-element.342, s32[]{:T(128)S(6)} %select_n.180, f32[2,32,2560]{2,1,0:T(8,128)S(1)} %get-tuple-element.356, f32[2,1280,768]{2,1,0:T(8,128)} %get-tuple-element.325, f32[2,1280,768]{2,1,0:T(8,128)} %get-tuple-element.326), kind=kOutput, calls=%fused_computation.19.clone.1 | convolution fusion | flops 1513881600 | bytes 16580612 | tf_op jit(solution)/shard_map/while/body/eval_jaxpr/lrk,lkw->lrw/dot_general | solution.py:82
  481.5 0.3 broadcast_multiply_fusion.6
  481.9 106.8 %select_multiply_fusion.3 = (f32[2,1280,768]{2,1,0:T(8,128)}, f32[2,1280,768]{2,1,0:T(8,128)}) fusion(f32[1280]{0:T(1024)S(1)} %compare_select_fusion.6, f32[2]{0:T(128)S(1)} %bitcast.107, pred[2]{0:T(512)(128)(4,1)S(1)} %broadcast_compare_fusion.6, s32[2]{0:T(128)S(1)} %compare_select_fusion.7, s32[1280,768]{1,0:T(8,128)S(1)} %broadcast_multiply_fusion.6, ...), kind=kLoop, calls=%fused_computation.11.clone.1 | loop fusion | flops 27525120 | bytes 19670034 | tf_op jit(solution)/shard_map/while/body/eval_jaxpr/mul | solution.py:45
  588.8 12.9 %fusion.41 = f32[2,32,5376]{2,1,0:T(8,128)S(1)} fusion(f32[2,32,5376]{2,1,0:T(8,128)S(1)} %get-tuple-element.342, s32[]{:T(128)S(6)} %select_n.180, f32[2,32,2560]{2,1,0:T(8,128)S(1)} %get-tuple-element.356, f32[2,1280,768]{2,1,0:T(8,128)} %get-tuple-element.325, f32[2,1280,768]{2,1,0:T(8,128)} %get-tuple-element.326), kind=kOutput, calls=%fused_computation.19.clone.1 | convolution fusion | flops 1513881600 | bytes 16580612 | tf_op jit(solution)/shard_map/while/body/eval_jaxpr/lrk,lkw->lrw/dot_general | solution.py:82
  601.8 0.3 broadcast_multiply_fusion.6
  602.2 106.8 %select_multiply_fusion.3 = (f32[2,1280,768]{2,1,0:T(8,128)}, f32[2,1280,768]{2,1,0:T(8,128)}) fusion(f32[1280]{0:T(1024)S(1)} %compare_select_fusion.6, f32[2]{0:T(128)S(1)} %bitcast.107, pred[2]{0:T(512)(128)(4,1)S(1)} %broadcast_compare_fusion.6, s32[2]{0:T(128)S(1)} %compare_select_fusion.7, s32[1280,768]{1,0:T(8,128)S(1)} %broadcast_multiply_fusion.6, ...), kind=kLoop, calls=%fused_computation.11.clone.1 | loop fusion | flops 27525120 | bytes 19670034 | tf_op jit(solution)/shard_map/while/body/eval_jaxpr/mul | solution.py:45
  709.1 12.9 %fusion.41 = f32[2,32,5376]{2,1,0:T(8,128)S(1)} fusion(f32[2,32,5376]{2,1,0:T(8,128)S(1)} %get-tuple-element.342, s32[]{:T(128)S(6)} %select_n.180, f32[2,32,2560]{2,1,0:T(8,128)S(1)} %get-tuple-element.356, f32[2,1280,768]{2,1,0:T(8,128)} %get-tuple-element.325, f32[2,1280,768]{2,1,0:T(8,128)} %get-tuple-element.326), kind=kOutput, calls=%fused_computation.19.clone.1 | convolution fusion | flops 1513881600 | bytes 16580612 | tf_op jit(solution)/shard_map/while/body/eval_jaxpr/lrk,lkw->lrw/dot_general | solution.py:82
  722.1 0.3 broadcast_multiply_fusion.6
  722.5 106.8 %select_multiply_fusion.3 = (f32[2,1280,768]{2,1,0:T(8,128)}, f32[2,1280,768]{2,1,0:T(8,128)}) fusion(f32[1280]{0:T(1024)S(1)} %compare_select_fusion.6, f32[2]{0:T(128)S(1)} %bitcast.107, pred[2]{0:T(512)(128)(4,1)S(1)} %broadcast_compare_fusion.6, s32[2]{0:T(128)S(1)} %compare_select_fusion.7, s32[1280,768]{1,0:T(8,128)S(1)} %broadcast_multiply_fusion.6, ...), kind=kLoop, calls=%fused_computation.11.clone.1 | loop fusion | flops 27525120 | bytes 19670034 | tf_op jit(solution)/shard_map/while/body/eval_jaxpr/mul | solution.py:45
  829.4 12.9 %fusion.41 = f32[2,32,5376]{2,1,0:T(8,128)S(1)} fusion(f32[2,32,5376]{2,1,0:T(8,128)S(1)} %get-tuple-element.342, s32[]{:T(128)S(6)} %select_n.180, f32[2,32,2560]{2,1,0:T(8,128)S(1)} %get-tuple-element.356, f32[2,1280,768]{2,1,0:T(8,128)} %get-tuple-element.325, f32[2,1280,768]{2,1,0:T(8,128)} %get-tuple-element.326), kind=kOutput, calls=%fused_computation.19.clone.1 | convolution fusion | flops 1513881600 | bytes 16580612 | tf_op jit(solution)/shard_map/while/body/eval_jaxpr/lrk,lkw->lrw/dot_general | solution.py:82
  842.4 0.3 broadcast_multiply_fusion.6
  842.8 106.8 %select_multiply_fusion.3 = (f32[2,1280,768]{2,1,0:T(8,128)}, f32[2,1280,768]{2,1,0:T(8,128)}) fusion(f32[1280]{0:T(1024)S(1)} %compare_select_fusion.6, f32[2]{0:T(128)S(1)} %bitcast.107, pred[2]{0:T(512)(128)(4,1)S(1)} %broadcast_compare_fusion.6, s32[2]{0:T(128)S(1)} %compare_select_fusion.7, s32[1280,768]{1,0:T(8,128)S(1)} %broadcast_multiply_fusion.6, ...), kind=kLoop, calls=%fused_computation.11.clone.1 | loop fusion | flops 27525120 | bytes 19670034 | tf_op jit(solution)/shard_map/while/body/eval_jaxpr/mul | solution.py:45
  949.7 12.9 %fusion.41 = f32[2,32,5376]{2,1,0:T(8,128)S(1)} fusion(f32[2,32,5376]{2,1,0:T(8,128)S(1)} %get-tuple-element.342, s32[]{:T(128)S(6)} %select_n.180, f32[2,32,2560]{2,1,0:T(8,128)S(1)} %get-tuple-element.356, f32[2,1280,768]{2,1,0:T(8,128)} %get-tuple-element.325, f32[2,1280,768]{2,1,0:T(8,128)} %get-tuple-element.326), kind=kOutput, calls=%fused_computation.19.clone.1 | convolution fusion | flops 1513881600 | bytes 16580612 | tf_op jit(solution)/shard_map/while/body/eval_jaxpr/lrk,lkw->lrw/dot_general | solution.py:82
  963.1 106.8 %select_multiply_fusion.3 = (f32[2,1280,768]{2,1,0:T(8,128)}, f32[2,1280,768]{2,1,0:T(8,128)}) fusion(f32[1280]{0:T(1024)S(1)} %compare_select_fusion.6, f32[2]{0:T(128)S(1)} %bitcast.107, pred[2]{0:T(512)(128)(4,1)S(1)} %broadcast_compare_fusion.6, s32[2]{0:T(128)S(1)} %compare_select_fusion.7, s32[1280,768]{1,0:T(8,128)S(1)} %broadcast_multiply_fusion.6, ...), kind=kLoop, calls=%fused_computation.11.clone.1 | loop fusion | flops 27525120 | bytes 19670034 | tf_op jit(solution)/shard_map/while/body/eval_jaxpr/mul | solution.py:45
  1070.0 12.9 %fusion.41 = f32[2,32,5376]{2,1,0:T(8,128)S(1)} fusion(f32[2,32,5376]{2,1,0:T(8,128)S(1)} %get-tuple-element.342, s32[]{:T(128)S(6)} %select_n.180, f32[2,32,2560]{2,1,0:T(8,128)S(1)} %get-tuple-element.356, f32[2,1280,768]{2,1,0:T(8,128)} %get-tuple-element.325, f32[2,1280,768]{2,1,0:T(8,128)} %get-tuple-element.326), kind=kOutput, calls=%fused_computation.19.clone.1 | convolution fusion | flops 1513881600 | bytes 16580612 | tf_op jit(solution)/shard_map/while/body/eval_jaxpr/lrk,lkw->lrw/dot_general | solution.py:82
  1082.9 1.0 slice_bitcast_fusion
  1084.1 25.9 %all-gather.1 = f32[16,2,5376]{2,1,0:T(2,128)S(1)} all-gather(f32[1,2,5376]{2,1,0:T(2,128)S(1)} %bitcast.106), channel_id=2, replica_groups=mesh['wave'=16,'lev'=16] {'lev'}, dimensions={0}, use_global_device_ids=true | all-gather | bytes 731136 | tf_op jit(solution)/shard_map/all_gather | solution.py:13
  1110.0 1.0 while.29
  1111.1 0.7 rev.10
  1112.1 0.7 rev.11
  1112.7 0.9 add_add_fusion
  (106 shorter events, 3.5 us)
Async XLA Ops:
  0.6 212.1 %copy-start = (s32[32]{0:T(128)S(1)}, s32[32]{0:T(128)}, u32[]{:S(2)}) copy-start(s32[32]{0:T(128)} %param.14) | copy-start | bytes 388
  11.1 7.8 copy-start.3
  11.1 7.9 copy-start.6
  11.1 143.2 %all-to-all-start = ((bf16[6,8,81,640]{2,1,0,3:T(8,128)(2,1)}), bf16[6,8,81,640]{2,1,0,3:T(8,128)(2,1)}, u32[]{:S(2)}, u32[]{:S(2)}) async-start(bf16[6,8,81,640]{2,1,0,3:T(8,128)(2,1)} %copy.44), calls=%async_computation | async-start | bytes 15728640 | tf_op jit(solution)/shard_map/all_to_all | solution.py:111
  200.3 12.4 %copy-start.8 = (s32[2]{0:T(128)S(1)}, s32[2]{0:T(128)}, u32[]{:S(2)}) copy-start(s32[2]{0:T(128)} %compare_select_fusion.3) | copy-start | bytes 28
  200.3 13.1 %copy-start.7 = (s32[32]{0:T(128)S(1)}, s32[32]{0:T(128)}, u32[]{:S(2)}) copy-start(s32[32]{0:T(128)} %param.15) | copy-start | bytes 388
  204.2 17.3 %all-to-all-start.1 = ((f32[16,1,7680]{2,1,0:T(1,128)}), f32[16,1,7680]{2,1,0:T(1,128)S(1)}, u32[]{:S(2)}, u32[]{:S(2)}) async-start(f32[16,1,7680]{2,1,0:T(1,128)} %reshape.245), calls=%async_computation.1 | async-start | bytes 983040 | tf_op jit(solution)/shard_map/all_to_all | solution.py:117
  227.2 856.7 %copy-start.4 = (f32[8]{0:T(128)S(1)}, f32[8]{0:T(128)}, u32[]{:S(2)}) copy-start(f32[8]{0:T(128)} %param.16) | copy-start | bytes 100
  1082.9 29.8 %copy-start.5 = (f32[8]{0:T(128)S(1)}, f32[8]{0:T(128)}, u32[]{:S(2)}) copy-start(f32[8]{0:T(128)} %param.17) | copy-start | bytes 100
  1082.9 30.7 %copy-start.1 = (s32[32]{0:T(128)S(1)}, s32[32]{0:T(128)}, u32[]{:S(2)}) copy-start(s32[32]{0:T(128)} %param.14) | copy-start | bytes 388
  1084.1 29.5 %copy-start.2 = (f32[2,8,5376]{2,1,0:T(8,128)}, f32[2,8,5376]{2,1,0:T(8,128)S(1)}, u32[]{:S(2)}) copy-start(f32[2,8,5376]{2,1,0:T(8,128)S(1)} %get-tuple-element.241) | copy-start | bytes 1032196
where the time goes:
time: 1120 us; the launch traced here: 1110 us
  other arithmetic  766 us (68%)
  waiting for transfers between devices  142 us (13%)
  matrix products  97.2 us (9%)
  local copies, waits for them, and re-layouts  50.9 us (5%)
  blocking collectives  25.9 us (2%)
  starting transfers between devices  16.3 us (1%)
  loops' own time  14.4 us (1%)
    mul x7, other arithmetic, synthesis_basis(): weights * jnp.cos(angles)  748 us
    all_to_all x1, waiting for transfers between devices, body(): lax.all_to_all(spectral, 'wave', split_axis=3, concat_axis=2, tiled=True)  134 us
    dot_general x7, matrix products, dense_block(): jnp.einsum('lrk,lkw->lrw', left_rows, basis_block, precision=lax.Precisio...  90.3 us
    all_to_all x2, local copies, waits for them, and re-layouts, body(): lax.all_to_all(spectral, 'wave', split_axis=3, concat_axis=2, tiled=True)  29.5 us
    all_gather x1, blocking collectives, entering(): pieces = lax.all_gather(value, axis)  25.9 us
  transfers between devices with their start and end apart: 2, of which 2 were waited for; matrix products, arithmetic and copies ran while one was open for 0% of the time, Pallas kernels for 0%

commit v1 on v0

v1 whole, which is shorter than its diff:
```python
import functools

import jax
import jax.numpy as jnp
from jax import lax
from jax.experimental import pallas as pl
from jax.experimental.pallas import tpu as pltpu
from jax.sharding import PartitionSpec as P

TRUNC = 1279
ROWS = 1281
LON_PAD = 5376
WAVES = 1280
STRIP = 768
STRIPS = LON_PAD // STRIP

COS_TERMS = (1.0, -19.73920440673828, 64.93911743164062, -85.45011138916016,
             60.16740036010742, -25.966703414916992, 6.5273566246032715)
SIN_TERMS = (6.2831854820251465, -41.34170150756836, 81.60513305664062, -76.7030029296875,
             42.02582931518555, -14.899463653564453, 3.2375807762145996)


def turn(product, circle):
    inverse = 1.0 / circle
    part = (product - jnp.floor(product * inverse + 0.5) * circle) * inverse
    square = part * part
    cosine = jnp.full_like(square, COS_TERMS[-1])
    sine = jnp.full_like(square, SIN_TERMS[-1])
    for term in COS_TERMS[-2::-1]:
        cosine = cosine * square + term
    for term in SIN_TERMS[-2::-1]:
        sine = sine * square + term
    return cosine, sine * part


def halves(value):
    high = value.astype(jnp.bfloat16)
    return high, (value - high.astype(jnp.float32)).astype(jnp.bfloat16)


def synthesis_kernel(counts, coef, waves_row, waves_column, entering, mixing,
                     out_v, out_d, out_t, out_s, out_h,
                     basis_high, basis_low, left_high, left_low, twist):
    circle_whole = counts[pl.program_id(0)]
    circle = jnp.full((1, 1), circle_whole, jnp.int32).astype(jnp.float32)

    def basis_rows(block, _):
        rows = pl.ds(pl.multiple_of(block * 16, 16), 16)
        other = pl.ds(pl.multiple_of(block * 16 + WAVES, 16), 16)
        column = lax.broadcasted_iota(jnp.int32, (16, STRIP), 1).astype(jnp.float32)
        cosine, sine = turn(waves_column[rows, :1] * column, circle)
        basis_high[rows, :], basis_low[rows, :] = halves(cosine)
        basis_high[other, :], basis_low[other, :] = halves(sine)
        return 0

    lax.fori_loop(0, WAVES // 16, basis_rows, 0)

    wave = waves_row[...]
    weight = jnp.where(2.0 * wave < circle, jnp.where(wave == 0.0, 1.0, 2.0), 0.0)
    start = (lax.broadcasted_iota(jnp.int32, (8, WAVES), 0) * STRIP).astype(jnp.float32)
    cosine, sine = turn(start * wave, circle)
    twist[0] = cosine * weight
    twist[1] = sine * weight
    factor = wave * (1.0 / (TRUNC + 1))

    def rows_of(field):
        if field < 3:
            return coef[0, 2 * field], coef[0, 2 * field + 1]
        real, imaginary = coef[0, 4], coef[0, 5]
        if field == 3:
            return -factor * imaginary, factor * real
        upper = []
        for value, side in ((real, 0), (imaginary, 1)):
            total = jnp.broadcast_to(entering[0, side : side + 1, :], (8, WAVES))
            for level in range(8):
                total = total + mixing[:, level : level + 1] * value[level : level + 1, :]
            upper.append(total)
        return upper[0], upper[1]

    for field in range(5):
        real, imaginary = rows_of(field)
        for strip in range(STRIPS):
            at = strip * 40 + field * 8
            cosine = twist[0, strip : strip + 1, :]
            sine = twist[1, strip : strip + 1, :]
            high, low = halves(real * cosine - imaginary * sine)
            left_high[at : at + 8, :WAVES] = high
            left_low[at : at + 8, :WAVES] = low
            high, low = halves(-(real * sine + imaginary * cosine))
            left_high[at : at + 8, WAVES:] = high
            left_low[at : at + 8, WAVES:] = low

    def block_of(block, _):
        first = pl.multiple_of(block * 256, 256)
        columns = pl.ds(first, 256)
        times = functools.partial(jnp.dot, preferred_element_type=jnp.float32)
        high = basis_high[:, columns]
        result = (times(left_high[...], high) + times(left_low[...], high)
                  + times(left_high[...], basis_low[:, columns]))
        lane = lax.broadcasted_iota(jnp.int32, (40, 256), 1) + first
        for strip in range(STRIPS):
            piece = jnp.where(lane + strip * STRIP < circle_whole,
                              result[strip * 40 : strip * 40 + 40], 0.0)
            where = pl.ds(pl.multiple_of(first + strip * STRIP, 256), 256)
            for field, out in enumerate((out_v, out_d, out_t, out_s, out_h)):
                out[0, :, where] = piece[field * 8 : field * 8 + 8]
        return 0

    lax.fori_loop(0, STRIP // 256, block_of, 0)


def synthesize(counts, coef, waves, entering, mixing):
    lats = coef.shape[0]
    whole = pl.BlockSpec(memory_space=pltpu.VMEM)
    grid_line = pl.BlockSpec((1, 8, LON_PAD), lambda i: (i, 0, 0))
    return pl.pallas_call(
        synthesis_kernel,
        grid=(lats,),
        out_shape=[jax.ShapeDtypeStruct((lats, 8, LON_PAD), jnp.float32)] * 5,
        in_specs=[
            pl.BlockSpec(memory_space=pltpu.SMEM),
            pl.BlockSpec((1, 6, 8, WAVES), lambda i: (i, 0, 0, 0)),
            whole,
            whole,
            pl.BlockSpec((1, 2, WAVES), lambda i: (i, 0, 0)),
            whole,
        ],
        out_specs=[grid_line] * 5,
        scratch_shapes=[
            pltpu.VMEM((2 * WAVES, STRIP), jnp.bfloat16),
            pltpu.VMEM((2 * WAVES, STRIP), jnp.bfloat16),
            pltpu.VMEM((STRIPS * 40 + 8, 2 * WAVES), jnp.bfloat16),
            pltpu.VMEM((STRIPS * 40 + 8, 2 * WAVES), jnp.bfloat16),
            pltpu.VMEM((2, 8, WAVES), jnp.float32),
        ],
        compiler_params=pltpu.CompilerParams(vmem_limit_bytes=50 * 2**20),
    )(counts, coef, waves[None, :], jnp.broadcast_to(waves[:, None], (WAVES, 128)), entering, mixing)


def legendre_split(spec_rows, polynomials, pair_ids):
    row_index = lax.broadcasted_iota(jnp.int32, (spec_rows.shape[2], spec_rows.shape[3]), 0)
    boundary = TRUNC + 1 - pair_ids[None, :]
    low_mask = row_index < boundary
    high_mask = (row_index >= boundary) & (row_index < ROWS)
    zero_value = jnp.zeros((), spec_rows.dtype)
    first_part = jnp.where(low_mask, spec_rows, zero_value)
    second_part = jnp.where(high_mask, spec_rows, zero_value)
    stacked = jnp.stack([first_part, second_part], 0)
    return jnp.einsum("hclrp,prq->qhclp", stacked, polynomials, preferred_element_type=jnp.float32)


def body(
    spectral, legendre, pair_list, lon_counts, lat_order, layer_depth_log, diagonal_layer_factor
):
    group_count = lax.axis_size("wave")
    group_index = lax.axis_index("wave")
    pair_share = pair_list.shape[0] // group_count
    lat_share = lat_order.shape[0] // group_count
    own_pairs = lax.dynamic_slice_in_dim(pair_list, group_index * pair_share, pair_share)
    own_lats = lax.dynamic_slice_in_dim(lat_order, group_index * lat_share, lat_share)
    chosen = own_lats[:, None] == jnp.arange(lat_order.shape[0])[None, :]
    own_counts = jnp.sum(jnp.where(chosen, lon_counts[None, :], 0), axis=1)
    waves = jnp.concatenate([pair_list, TRUNC - pair_list]).astype(jnp.float32)

    slots = (jnp.arange(lat_order.shape[0])[:, None] == lat_order[None, :]).astype(jnp.bfloat16)
    polynomials = jnp.einsum(
        "prq,qi->pri", legendre, slots, preferred_element_type=jnp.float32
    ).astype(jnp.bfloat16)
    values = legendre_split(
        lax.all_to_all(spectral, "wave", split_axis=3, concat_axis=2, tiled=True),
        polynomials,
        own_pairs,
    )
    fourier = lax.all_to_all(values, "wave", split_axis=0, concat_axis=4, tiled=True)
    coef = jnp.transpose(fourier, (0, 2, 3, 1, 4)).reshape(lat_share, 6, 8, WAVES)

    scaled = jnp.sum(layer_depth_log[None, None, :, None] * coef[:, 4:], axis=2)
    pieces = lax.all_gather(scaled, "lev")
    later = jnp.arange(pieces.shape[0]) > lax.axis_index("lev")
    entering = jnp.sum(jnp.where(later[:, None, None, None], pieces, 0.0), axis=0)
    level = jnp.arange(8)
    mixing = jnp.where(
        level[None, :] == level[:, None],
        diagonal_layer_factor[:, None],
        jnp.where(level[None, :] > level[:, None], layer_depth_log[None, :], 0.0),
    )
    return tuple(synthesize(own_counts, coef, waves, entering, mixing))


def solution(mesh):
    placed = (
        P(None, "lev", "wave", None),
        P("wave", None, None),
        P(),
        P(),
        P(),
        P("lev"),
        P("lev"),
    )
    return jax.shard_map(
        body,
        mesh=mesh,
        in_specs=placed,
        out_specs=(P("wave", "lev", None),) * 5,
        check_vma=False,
    )
```

time: 1120 us -> 286 us (0.26)
  other arithmetic: 766 us -> 12 us
  matrix products: 97.2 us -> 7.31 us
  Pallas kernels: 0 us -> 34.3 us
  loops' own time: 14.4 us -> 0 us
    mul x23 -> x0, other arithmetic: 750 us -> none  [the longest x7 748 us: synthesis_basis(): weights * jnp.cos(angles)]
    dot_general x7 -> x0, matrix products: 90.3 us -> none  [dense_block(): jnp.einsum('lrk,lkw->lrw', left_rows, basis_block, precision=lax.Precisio...]
    pallas_call x0 -> x1, Pallas kernels: none -> 34.3 us  [synthesize(): pl.pallas_call(synthesis_kernel, grid=(lats,), out_shape=[jax.ShapeDtypeS...]
    another operation x2 -> x0, loops' own time: 14.4 us -> none  [the longest x1 14.1 us: synthesize(): grid_full = lax.fori_loop(0, LON_PAD // 768, dense_block, grid_empty)]
  transfers between devices with their start and end apart: 2 -> 2, of which waited for: 2 -> 2; matrix products, arithmetic and copies ran while one was open for 0% -> 1% of each run, Pallas kernels for 0% -> 0%
where the time goes in v1:
time: 286 us; the launch traced here: 285 us
  waiting for transfers between devices  142 us (50%)
  local copies, waits for them, and re-layouts  47.2 us (17%)
  Pallas kernels  34.3 us (12%)
  blocking collectives  24.9 us (9%)
  starting transfers between devices  16.4 us (6%)
  other arithmetic  12 us (4%)
  matrix products  7.31 us (3%)
    all_to_all x1, waiting for transfers between devices, body(): lax.all_to_all(spectral, 'wave', split_axis=3, concat_axis=2, tiled=True)  134 us
    pallas_call x1, Pallas kernels, synthesize(): pl.pallas_call(synthesis_kernel, grid=(lats,), out_shape=[jax.ShapeDtypeS...  34.3 us
    all_to_all x2, local copies, waits for them, and re-layouts, body(): lax.all_to_all(spectral, 'wave', split_axis=3, concat_axis=2, tiled=True)  29.2 us
    all_gather x1, blocking collectives, body(): pieces = lax.all_gather(scaled, 'lev')  24.9 us
    unnamed x13, local copies, waits for them, and re-layouts  14.1 us
    all_to_all x1, starting transfers between devices, body(): lax.all_to_all(values, 'wave', split_axis=0, concat_axis=4, tiled=True)  8.67 us
    select_n x1, other arithmetic, legendre_split(): first_part = jnp.where(low_mask, spec_rows, zero_value)  8.16 us
    all_to_all x1, waiting for transfers between devices, body(): lax.all_to_all(values, 'wave', split_axis=0, concat_axis=4, tiled=True)  8 us
  transfers between devices with their start and end apart: 2, of which 2 were waited for; matrix products, arithmetic and copies ran while one was open for 1% of the time, Pallas kernels for 0%

profile of v1, /device:TPU:1, one launch (start us, length us, event | category | flops | bytes accessed | tf_op | source)
XLA Modules:
  0.0 285.3 jit_solution(9996118393018448382)
XLA Ops:
  0.6 10.5 %copy.28 = bf16[6,8,81,640]{2,1,0,3:T(8,128)(2,1)} copy(bf16[6,8,81,640]{3,1,2,0:T(8,128)(2,1)} %param.7) | data formatting | bytes 9953280 | tf_op args[0]
  11.1 0.0 copy-start.4
  11.1 0.0 copy-start
  11.1 0.0 copy-start.3
  11.1 7.8 %all-to-all-start = ((bf16[6,8,81,640]{2,1,0,3:T(8,128)(2,1)}), bf16[6,8,81,640]{2,1,0,3:T(8,128)(2,1)}, u32[]{:S(2)}, u32[]{:S(2)}) async-start(bf16[6,8,81,640]{2,1,0,3:T(8,128)(2,1)} %copy.28), calls=%async_computation | async-start | bytes 15728640 | tf_op jit(solution)/shard_map/all_to_all | solution.py:170
  18.9 0.0 copy-done.4
  18.9 0.1 dynamic_slice.6
  19.0 0.0 copy-done
  19.0 0.1 dynamic-slice_subtract_fusion
  19.1 0.6 add_convert_fusion
  19.7 0.0 copy-done.3
  19.7 0.2 fusion.17.counts
  19.9 0.1 iota_compare_fusion.1
  20.0 134.3 %all-to-all-done = bf16[6,8,81,640]{2,1,0,3:T(8,128)(2,1)} async-done(((bf16[6,8,81,640]{2,1,0,3:T(8,128)(2,1)}), bf16[6,8,81,640]{2,1,0,3:T(8,128)(2,1)}, u32[]{:S(2)}, u32[]{:S(2)}) %all-to-all-start) | async-done | bytes 4976672 | tf_op jit(solution)/shard_map/all_to_all | solution.py:170
  154.4 15.5 %copy.30 = bf16[6,8,16,81,40]{3,2,1,0,4:T(8,128)(2,1)} copy(bf16[6,8,16,81,40]{3,1,0,4,2:T(8,128)(2,1)} %bitcast.6) | data formatting | bytes 9953280 | tf_op jit(solution)/shard_map/all_to_all | solution.py:170
  169.9 13.7 %all_to_all.29 = bf16[1,6,8,1296,40]{3,2,1,0,4:T(8,128)(2,1)} reshape(bf16[6,8,16,81,40]{3,2,1,0,4:T(8,128)(2,1)} %copy.30) | data formatting | bytes 9953280 | tf_op jit(solution)/shard_map/all_to_all | solution.py:170
  183.6 8.2 %broadcast_select_fusion.1 = (bf16[1,6,8,1296,40]{3,2,1,0,4:T(8,128)(2,1)}, bf16[1,6,8,1296,40]{3,2,1,0,4:T(8,128)(2,1)}) fusion(bf16[1,6,8,1296,40]{3,2,1,0,4:T(8,128)(2,1)} %all_to_all.29, pred[1296,40]{0,1:T(8,128)(4,1)S(1)} %get-tuple-element.7, pred[1296,40]{0,1:T(8,128)(4,1)S(1)} %get-tuple-element.8), kind=kLoop, calls=%fused_computation.5 | loop fusion | flops 4976640 | bytes 15033600 | tf_op jit(solution)/shard_map/jit(_where)/select_n | solution.py:146
  191.7 7.3 %fusion.5 = f32[32,2,6,8,40]{0,3,2,1,4:T(8,128)S(1)} fusion(bf16[1,6,8,1296,40]{3,2,1,0,4:T(8,128)(2,1)} %get-tuple-element.6, bf16[1,6,8,1296,40]{3,2,1,0,4:T(8,128)(2,1)} %get-tuple-element.5, bf16[40,1296,32]{1,2,0:T(8,128)(2,1)} %param.8, s32[32]{0:T(128)S(1)} %copy-done.4), kind=kOutput, calls=%fused_computation.8 | convolution fusion | flops 446239744 | bytes 13762688 | tf_op jit(solution)/shard_map/hclrp,prq->qhclp/dot_general | solution.py:149
  199.1 0.0 copy-start.2
  199.1 1.4 copy.31
  200.4 2.3 reshape.93
  202.7 0.0 copy-start.1
  202.7 8.7 %all-to-all-start.1 = ((f32[16,1,7680]{2,1,0:T(1,128)}), f32[16,1,7680]{2,1,0:T(1,128)S(1)}, u32[]{:S(2)}, u32[]{:S(2)}) async-start(f32[16,1,7680]{2,1,0:T(1,128)} %reshape.93), calls=%async_computation.1 | async-start | bytes 983040 | tf_op jit(solution)/shard_map/all_to_all | solution.py:174
  211.5 0.0 copy-done.2
  211.5 0.7 select_select_fusion.mixing
  212.2 8.0 %all-to-all-done.1 = f32[16,1,7680]{2,1,0:T(1,128)S(1)} async-done(((f32[16,1,7680]{2,1,0:T(1,128)}), f32[16,1,7680]{2,1,0:T(1,128)S(1)}, u32[]{:S(2)}, u32[]{:S(2)}) %all-to-all-start.1) | async-done | bytes 491552 | tf_op jit(solution)/shard_map/all_to_all | solution.py:174
  220.2 0.5 broadcast.42
  220.7 1.8 reduce
  222.5 1.3 reshape.94
  223.8 0.9 copy.32
  224.7 0.8 all_to_all.33
  225.5 0.1 fusion.11
  225.7 24.9 %all-gather = f32[32,2,1280]{2,1,0:T(2,128)S(1)} all-gather(f32[2,2,1280]{2,1,0:T(2,128)S(1)} %fusion.11), channel_id=2, replica_groups=mesh['wave'=16,'lev'=16] {'lev'}, dimensions={0}, use_global_device_ids=true | all-gather | bytes 348160 | tf_op jit(solution)/shard_map/all_gather | solution.py:178
  250.5 0.2 select_reduce_fusion.entering
  250.8 0.0 copy-done.1
  250.8 0.2 broadcast_in_dim.82.waves_column
  251.0 34.3 %shard_map.110 = (f32[2,8,5376]{2,1,0:T(8,128)}, f32[2,8,5376]{2,1,0:T(8,128)}, f32[2,8,5376]{2,1,0:T(8,128)}, f32[2,8,5376]{2,1,0:T(8,128)}, f32[2,8,5376]{2,1,0:T(8,128)}) custom-call(s32[2]{0:T(128)S(1)} %fusion.17.counts, f32[2,6,8,1280]{3,2,1,0:T(8,128)S(1)} %bitcast.32, f32[1,1280]{1,0:T(1,128)S(1)} %add_convert_fusion.1.waves_row, ...), custom_call_target="tpu_custom_call" | custom-call | tf_op jit(solution)/shard_map/pallas_call | solution.py:116
  (7 shorter events, 0.1 us)
Async XLA Ops:
  11.1 7.8 %copy-start.4 = (s32[32]{0:T(128)S(1)}, s32[32]{0:T(128)}, u32[]{:S(2)}) copy-start(s32[32]{0:T(128)} %param.11) | copy-start | bytes 388
  11.1 7.9 %copy-start = (s32[640]{0:T(1024)S(1)}, s32[640]{0:T(1024)}, u32[]{:S(2)}) copy-start(s32[640]{0:T(1024)} %param.9) | copy-start | bytes 7684
  11.1 8.6 %copy-start.3 = (s32[32]{0:T(128)S(1)}, s32[32]{0:T(128)}, u32[]{:S(2)}) copy-start(s32[32]{0:T(128)} %param.10) | copy-start | bytes 388
  11.1 143.2 %all-to-all-start = ((bf16[6,8,81,640]{2,1,0,3:T(8,128)(2,1)}), bf16[6,8,81,640]{2,1,0,3:T(8,128)(2,1)}, u32[]{:S(2)}, u32[]{:S(2)}) async-start(bf16[6,8,81,640]{2,1,0,3:T(8,128)(2,1)} %copy.28), calls=%async_computation | async-start | bytes 15728640 | tf_op jit(solution)/shard_map/all_to_all | solution.py:170
  199.1 12.4 %copy-start.2 = (f32[8]{0:T(128)S(1)}, f32[8]{0:T(128)}, u32[]{:S(2)}) copy-start(f32[8]{0:T(128)} %param.12) | copy-start | bytes 100
  202.7 48.0 %copy-start.1 = (f32[1280]{0:T(1024)S(1)}, f32[1280]{0:T(1024)}, u32[]{:S(2)}) copy-start(f32[1280]{0:T(1024)} %add_convert_fusion) | copy-start | bytes 15364
  202.7 17.5 %all-to-all-start.1 = ((f32[16,1,7680]{2,1,0:T(1,128)}), f32[16,1,7680]{2,1,0:T(1,128)S(1)}, u32[]{:S(2)}, u32[]{:S(2)}) async-start(f32[16,1,7680]{2,1,0:T(1,128)} %reshape.93), calls=%async_computation.1 | async-start | bytes 983040 | tf_op jit(solution)/shard_map/all_to_all | solution.py:174

commit v2 on v1

v2 whole, which is shorter than its diff:
```python
import functools

import jax
import jax.numpy as jnp
from jax import lax
from jax.experimental import pallas as pl
from jax.experimental.pallas import tpu as pltpu
from jax.sharding import PartitionSpec as P

TRUNC = 1279
ROWS = 1281
LON_PAD = 5376
WAVES = 1280
STRIP = 768
STRIPS = LON_PAD // STRIP
PEERS = 16
SHARE = 40
HALVES = (320, 328)
ORDER = ((2, 2), (1, 0), (3, 0), (0, 1), (0, 3), (1, 2), (3, 2), (2, 1), (2, 3), (2, 0), (0, 2),
         (1, 1), (3, 3), (1, 3), (3, 1))
MESH = pl.DeviceIdType.MESH

COS_TERMS = (1.0, -19.73920440673828, 64.93911743164062, -85.45011138916016,
             60.16740036010742, -25.966703414916992, 6.5273566246032715)
SIN_TERMS = (6.2831854820251465, -41.34170150756836, 81.60513305664062, -76.7030029296875,
             42.02582931518555, -14.899463653564453, 3.2375807762145996)


def turn(product, circle):
    inverse = 1.0 / circle
    part = (product - jnp.floor(product * inverse + 0.5) * circle) * inverse
    square = part * part
    cosine = jnp.full_like(square, COS_TERMS[-1])
    sine = jnp.full_like(square, SIN_TERMS[-1])
    for term in COS_TERMS[-2::-1]:
        cosine = cosine * square + term
    for term in SIN_TERMS[-2::-1]:
        sine = sine * square + term
    return cosine, sine * part


def halves(value):
    high = value.astype(jnp.bfloat16)
    return high, (value - high.astype(jnp.float32)).astype(jnp.bfloat16)


def exchange_kernel(pairs, lon_counts, lat_order, depth, spectral, legendre, pair_row, slots,
                    out_fourier, out_above, out_basis,
                    spec, legs, send_a, send_b, got_a, got_b, stage, rights, lefts, shuffle,
                    summed, send_f, got_f, send_c, got_c, column, table,
                    in_sem, leg_sem, spec_send, spec_recv, spec_own, four_send, four_recv, four_own,
                    lev_send, lev_recv, table_sem):
    wave, lev = lax.axis_index("wave"), lax.axis_index("lev")
    across, along = wave // 4, lax.rem(wave, 4)
    times = functools.partial(jnp.dot, preferred_element_type=jnp.float32)

    loads = []
    for part in (1, 0):
        load = pltpu.make_async_copy(spectral.at[pl.ds(3 * part, 3)], spec.at[pl.ds(3 * part, 3)],
                                     in_sem.at[part])
        load.start()
        loads.append(load)
    leg_load = pltpu.make_async_copy(legendre, legs, leg_sem)
    leg_load.start()

    barrier = pltpu.get_barrier_semaphore()
    for step in range(1, PEERS):
        pl.semaphore_signal(barrier, inc=1, device_id=(lax.rem(wave + step, PEERS), lev),
                            device_id_type=MESH)
        pl.semaphore_signal(barrier, inc=1, device_id=(wave, lax.rem(lev + step, PEERS)),
                            device_id_type=MESH)

    def window(duo):
        return jnp.minimum((80 * duo) // 128, 3) * 128

    def shuffle_rows(duo, _):
        lane = lax.broadcasted_iota(jnp.int32, (1, 256), 1)
        second = jnp.where(lane >= 128, 1, 0)
        inner = lane - 128 * second
        third = jnp.where(inner >= 40, 1, 0) + jnp.where(inner >= 80, 1, 0) + jnp.where(inner >= 120, 1, 0)
        source = 80 * duo - window(duo) + 40 * second + inner - 40 * third
        row = lax.broadcasted_iota(jnp.int32, (256, 256), 0)
        for place in range(3):
            wanted = jnp.where(third == place, source, -1)
            shuffle[duo, place] = jnp.where(row == wanted, 1.0, 0.0).astype(jnp.bfloat16)
        return 0

    lax.fori_loop(0, 8, shuffle_rows, 0)
    pl.semaphore_wait(barrier, 2 * (PEERS - 1))

    copies = []
    waits = {}
    for part in (1, 0):
        loads[1 - part].wait()
        for half, (rows, send, got) in enumerate(zip(HALVES, (send_a, send_b), (got_a, got_b))):
            first = half * HALVES[0]

            def shuffled(duo, _, part=part, first=first, rows=rows, send=send):
                lanes = pl.ds(pl.multiple_of(window(duo), 128), 256)
                total = times(spec[3 * part, first : first + rows, lanes], shuffle[duo, 0])
                for place in (1, 2):
                    total = total + times(spec[3 * part + place, first : first + rows, lanes],
                                          shuffle[duo, place])
                send[part, 2 * duo] = total[:, :128].astype(jnp.bfloat16)
                send[part, 2 * duo + 1] = total[:, 128:].astype(jnp.bfloat16)
                return 0

            lax.fori_loop(0, 8, shuffled, 0)
            here = []
            for number, (x, y) in enumerate(ORDER):
                other = lax.rem(across + x, 4) * 4 + lax.rem(along + y, 4)
                copy = pltpu.make_async_remote_copy(
                    src_ref=send.at[part, other], dst_ref=got.at[part, wave],
                    send_sem=spec_send.at[part, half, number], recv_sem=spec_recv.at[part, half, number],
                    device_id=(other, lev), device_id_type=MESH)
                copy.start()
                here.append(copy)
            own = pltpu.make_async_copy(send.at[part, wave], got.at[part, wave], spec_own.at[part, half])
            own.start()
            waits[part, half] = (here, own)
            copies += here

    leg_load.wait()

    def masked(place, _):
        boundary = TRUNC + 1 - pairs[wave * SHARE + place]
        values = legs[place].astype(jnp.float32)
        row = lax.broadcasted_iota(jnp.int32, values.shape, 1)
        low = jnp.where(row < boundary, values, 0.0)
        high = jnp.where((row >= boundary) & (row < ROWS), values, 0.0)
        lefts[pl.ds(pl.multiple_of(place * 64, 64), 32), :] = low.astype(jnp.bfloat16)
        lefts[pl.ds(pl.multiple_of(place * 64 + 32, 32), 32), :] = high.astype(jnp.bfloat16)
        return 0

    lax.fori_loop(0, SHARE, masked, 0)
    column[...] = jnp.transpose(jnp.broadcast_to(pair_row[...].astype(jnp.float32), (128, 640)))

    def table_copy(lat, block):
        slot = lax.rem(block, 2)
        return pltpu.make_async_copy(
            table.at[slot], out_basis.at[lat, :, :, pl.ds(pl.multiple_of(block * 128, 128), 128), :],
            table_sem.at[slot])

    def tables(lat):
        whole = lon_counts[lat_order[2 * wave + lat]]
        circle = jnp.full((1, 1), whole, jnp.int32).astype(jnp.float32)

        def block_of(block, _):
            slot = lax.rem(block, 2)

            @pl.when(block >= 2)
            def _():
                table_copy(lat, block - 2).wait()

            low = block < 5
            at = (block - jnp.where(low, 0, 5)) * 128
            base = jnp.where(low, 0.0, float(TRUNC))
            sign = jnp.where(low, 1.0, -1.0)

            def rows_of(step, _):
                rows = pl.ds(pl.multiple_of(step * 16, 16), 16)
                strip = lax.broadcasted_iota(jnp.int32, (16, STRIP), 1).astype(jnp.float32)
                source = column[pl.ds(pl.multiple_of(at + step * 16, 16), 16), :]
                number = jnp.concatenate([base + sign * source] * (STRIP // 128), axis=1)
                cosine, sine = turn(number * strip, circle)
                table[slot, 0, 0, rows, :], table[slot, 1, 0, rows, :] = halves(cosine)
                table[slot, 0, 1, rows, :], table[slot, 1, 1, rows, :] = halves(sine)
                return 0

            lax.fori_loop(0, 8, rows_of, 0)
            table_copy(lat, block).start()
            return 0

        lax.fori_loop(0, 10, block_of, 0)
        table_copy(lat, 8).wait()
        table_copy(lat, 9).wait()

    def legendre_sums(part):
        for half in (0, 1):
            here, own = waits[part, half]
            for copy in here:
                copy.wait_recv()
            own.wait()

        def widen(source, _):
            stage[pl.ds(pl.multiple_of(source * 648, 8), 320), :] = got_a[part, source].astype(jnp.float32)
            stage[pl.ds(pl.multiple_of(source * 648 + 320, 8), 328), :] = got_b[part, source].astype(jnp.float32)
            return 0

        lax.fori_loop(0, PEERS, widen, 0)

        def gather(chunk, _):
            rows = pl.ds(pl.multiple_of(chunk * 144, 16), 144)
            for level in range(8):
                taken = stage[pl.ds(chunk * 1152 + level, 144, stride=8), :]
                lanes = slice(128 * (level % 2), 128 * (level % 2) + 128)
                rights[level // 2, rows, lanes] = taken.astype(jnp.bfloat16)
            return 0

        lax.fori_loop(0, 9, gather, 0)
        lane = lax.broadcasted_iota(jnp.int32, (1, 256), 1)
        inner = jnp.where(lane >= 128, lane - 128, lane)
        inner = jnp.where(inner >= 80, inner - 80, jnp.where(inner >= 40, inner - 40, inner))

        def levels(duo, _):
            def group(chunk, total):
                result = times(lefts[pl.ds(pl.multiple_of(chunk * 512, 512), 512), :], rights[duo])
                for place in range(8):
                    total = total + jnp.where(inner == chunk * 8 + place,
                                              result[place * 64 : place * 64 + 64], 0.0)
                return total

            summed[duo] = lax.fori_loop(0, 5, group, jnp.zeros((64, 256), jnp.float32))
            return 0

        lax.fori_loop(0, 4, levels, 0)
        for duo in range(4):
            rest = summed[duo]
            moved = jnp.zeros((64, 256), jnp.float32)
            for _ in range(3):
                piece = rest.astype(jnp.bfloat16)
                rest = rest - piece.astype(jnp.float32)
                moved = moved + times(slots[...], piece)
            send_f[part, pl.ds(2 * duo, 64, stride=8), :] = moved[:, :128]
            send_f[part, pl.ds(2 * duo + 1, 64, stride=8), :] = moved[:, 128:]
        here = []
        for number, (x, y) in enumerate(ORDER):
            other = lax.rem(across + x, 4) * 4 + lax.rem(along + y, 4)
            copy = pltpu.make_async_remote_copy(
                src_ref=send_f.at[part, pl.ds(pl.multiple_of(other * 32, 32), 32), :],
                dst_ref=got_f.at[part, pl.ds(pl.multiple_of(wave * 32, 32), 32), :],
                send_sem=four_send.at[part, number], recv_sem=four_recv.at[part, number],
                device_id=(other, lev), device_id_type=MESH)
            copy.start()
            here.append(copy)
        own = pltpu.make_async_copy(
            send_f.at[part, pl.ds(pl.multiple_of(wave * 32, 32), 32), :],
            got_f.at[part, pl.ds(pl.multiple_of(wave * 32, 32), 32), :], four_own.at[part])
        own.start()
        copies.extend(here)
        return here, own

    def arrived(here, own):
        for copy in here:
            copy.wait_recv()
        own.wait()

    tables(0)
    tables(1)
    first = legendre_sums(1)
    arrived(*first)
    level = lax.broadcasted_iota(jnp.int32, (1, 8, 128), 1)
    share = jnp.zeros((1, 8, 128), jnp.float32)
    for number in range(8):
        share = jnp.where(level == number, depth[number], share)
    send_c[...] = jnp.sum(got_f[1].reshape(64, 8, 128) * share, axis=1)
    lev_copies = []
    for step in range(1, PEERS):
        copy = pltpu.make_async_remote_copy(
            src_ref=send_c, dst_ref=got_c.at[lev],
            send_sem=lev_send.at[step - 1], recv_sem=lev_recv.at[step - 1],
            device_id=(wave, lax.rem(lev + step, PEERS)), device_id_type=MESH)
        copy.start()
        lev_copies.append(copy)
    out_fourier[1] = got_f[1]
    second = legendre_sums(0)
    for copy in lev_copies:
        copy.wait_recv()
    above = jnp.zeros((64, 128), jnp.float32)
    got_c[lev] = send_c[...]
    for other in range(PEERS):
        above = above + jnp.where(other > lev, got_c[other], 0.0)
    out_above[...] = above
    arrived(*second)
    out_fourier[0] = got_f[0]
    for copy in copies + lev_copies:
        copy.wait_send()


def exchange(pairs, lon_counts, lat_order, depth, spectral, legendre, pair_row, slots):
    anywhere = pl.BlockSpec(memory_space=pl.ANY)
    vector = pl.BlockSpec(memory_space=pltpu.VMEM)
    scalar = pl.BlockSpec(memory_space=pltpu.SMEM)
    dma = pltpu.SemaphoreType.DMA
    return pl.pallas_call(
        exchange_kernel,
        out_shape=[
            jax.ShapeDtypeStruct((2, 512, 128), jnp.float32),
            jax.ShapeDtypeStruct((64, 128), jnp.float32),
            jax.ShapeDtypeStruct((2, 2, 2, WAVES, STRIP), jnp.bfloat16),
        ],
        in_specs=[scalar] * 4 + [anywhere] * 2 + [vector] * 2,
        out_specs=[vector, vector, anywhere],
        scratch_shapes=[
            pltpu.VMEM((6, 648, 640), jnp.bfloat16),
            pltpu.VMEM((SHARE, 32, 1296), jnp.bfloat16),
            pltpu.VMEM((2, PEERS, HALVES[0], 128), jnp.bfloat16),
            pltpu.VMEM((2, PEERS, HALVES[1], 128), jnp.bfloat16),
            pltpu.VMEM((2, PEERS, HALVES[0], 128), jnp.bfloat16),
            pltpu.VMEM((2, PEERS, HALVES[1], 128), jnp.bfloat16),
            pltpu.VMEM((PEERS * 648, 128), jnp.float32),
            pltpu.VMEM((4, 1296, 256), jnp.bfloat16),
            pltpu.VMEM((SHARE * 64, 1296), jnp.bfloat16),
            pltpu.VMEM((8, 3, 256, 256), jnp.bfloat16),
            pltpu.VMEM((4, 64, 256), jnp.float32),
            pltpu.VMEM((2, 512, 128), jnp.float32),
            pltpu.VMEM((2, 512, 128), jnp.float32),
            pltpu.VMEM((64, 128), jnp.float32),
            pltpu.VMEM((PEERS, 64, 128), jnp.float32),
            pltpu.VMEM((640, 128), jnp.float32),
            pltpu.VMEM((2, 2, 2, 128, STRIP), jnp.bfloat16),
            dma((2,)), dma, dma((2, 2, 15)), dma((2, 2, 15)), dma((2, 2)),
            dma((2, 15)), dma((2, 15)), dma((2,)), dma((15,)), dma((15,)), dma((2,)),
        ],
        compiler_params=pltpu.CompilerParams(
            collective_id=0, has_side_effects=True, vmem_limit_bytes=56 * 2**20
        ),
    )(pairs, lon_counts, lat_order, depth, spectral, legendre, pair_row, slots)


def synthesis_kernel(lon_counts, lat_order, depth, diagonal, fourier, above, pair_row, basis,
                     out_v, out_d, out_t, out_s, out_h,
                     table, left_high, left_low, twist, coef, upper, table_sem):
    lat = pl.program_id(0)
    wave_group = lax.axis_index("wave")

    def load(which):
        return pltpu.make_async_copy(basis.at[which], table.at[which], table_sem.at[which])

    @pl.when(lat == 0)
    def _():
        load(0).start()
        load(1).start()

    circle_whole = lon_counts[lat_order[2 * wave_group + lat]]
    circle = jnp.full((1, 1), circle_whole, jnp.int32).astype(jnp.float32)
    lane = lax.broadcasted_iota(jnp.int32, (1, 128), 1)

    def spread(take, keep, height):
        for place in range(3):
            tiles = [jnp.zeros((height, 128), jnp.float32)] * 5
            for source in range(PEERS):
                value = take(source)
                goal = source * SHARE
                tile, offset = goal // 128, goal % 128
                rolled = pltpu.roll(value, (offset - place * SHARE) % 128, 1)
                end = offset + SHARE
                tiles[tile] = jnp.where((lane >= offset) & (lane < end), rolled, tiles[tile])
                if end > 128:
                    tiles[tile + 1] = jnp.where(lane < end - 128, rolled, tiles[tile + 1])
            for tile in range(5):
                keep(place, tile, tiles[tile])

    for part in range(2):
        for side in range(2):
            def take(source, part=part, side=side):
                return fourier[part, pl.ds(pl.multiple_of(source * 32 + lat * 16 + side * 8, 8), 8), :]

            def keep(place, tile, value, part=part, side=side):
                at = side * 640 + tile * 128
                coef[3 * part + place, :, at : at + 128] = value

            spread(take, keep, 8)

    def take_above(source):
        return above[source]

    def keep_above(place, tile, value):
        upper[place, :, tile * 128 : tile * 128 + 128] = value

    spread(take_above, keep_above, 4)

    pair = pair_row[...].astype(jnp.float32)
    wave = jnp.concatenate([pair, TRUNC - pair], axis=1)
    weight = jnp.where(2.0 * wave < circle, jnp.where(wave == 0.0, 1.0, 2.0), 0.0)
    start = (lax.broadcasted_iota(jnp.int32, (8, WAVES), 0) * STRIP).astype(jnp.float32)
    cosine, sine = turn(start * wave, circle)
    twist[0] = cosine * weight
    twist[1] = sine * weight
    factor = wave * (1.0 / (TRUNC + 1))
    level_of = lax.broadcasted_iota(jnp.int32, (8, 1), 0)

    def rows_of(field):
        if field < 3:
            return coef[2 * field], coef[2 * field + 1]
        real, imaginary = coef[4], coef[5]
        if field == 3:
            return -factor * imaginary, factor * real
        higher = []
        for value, place in ((real, 1), (imaginary, 2)):
            total = jnp.broadcast_to(
                jnp.concatenate([upper[place, pl.ds(2 * lat, 1), :], upper[place, pl.ds(2 * lat + 1, 1), :]], axis=1),
                (8, WAVES))
            for level in range(8):
                share = jnp.where(level_of == level, diagonal[level],
                                  jnp.where(level_of < level, depth[level], 0.0))
                total = total + share * value[level : level + 1, :]
            higher.append(total)
        return higher[0], higher[1]

    for field in range(5):
        real, imaginary = rows_of(field)
        for strip in range(STRIPS):
            at = strip * 40 + field * 8
            cosine = twist[0, strip : strip + 1, :]
            sine = twist[1, strip : strip + 1, :]
            high, low = halves(real * cosine - imaginary * sine)
            left_high[0, at : at + 8, :] = high
            left_low[0, at : at + 8, :] = low
            high, low = halves(-(real * sine + imaginary * cosine))
            left_high[1, at : at + 8, :] = high
            left_low[1, at : at + 8, :] = low

    load(lat).wait()

    def block_of(block, _):
        first = pl.multiple_of(block * 256, 256)
        columns = pl.ds(first, 256)
        times = functools.partial(jnp.dot, preferred_element_type=jnp.float32)
        result = None
        for trig in (0, 1):
            high = table[lat, 0, trig, :, columns]
            term = (times(left_high[trig], high) + times(left_low[trig], high)
                    + times(left_high[trig], table[lat, 1, trig, :, columns]))
            result = term if result is None else result + term
        number = lax.broadcasted_iota(jnp.int32, (40, 256), 1) + first
        for strip in range(STRIPS):
            piece = jnp.where(number + strip * STRIP < circle_whole,
                              result[strip * 40 : strip * 40 + 40], 0.0)
            where = pl.ds(pl.multiple_of(first + strip * STRIP, 256), 256)
            for field, out in enumerate((out_v, out_d, out_t, out_s, out_h)):
                out[0, :, where] = piece[field * 8 : field * 8 + 8]
        return 0

    lax.fori_loop(0, STRIP // 256, block_of, 0)


def synthesize(lon_counts, lat_order, depth, diagonal, fourier, above, pair_row, basis):
    whole = pl.BlockSpec(memory_space=pltpu.VMEM)
    scalar = pl.BlockSpec(memory_space=pltpu.SMEM)
    grid_line = pl.BlockSpec((1, 8, LON_PAD), lambda i: (i, 0, 0))
    return pl.pallas_call(
        synthesis_kernel,
        grid=(2,),
        out_shape=[jax.ShapeDtypeStruct((2, 8, LON_PAD), jnp.float32)] * 5,
        in_specs=[scalar] * 4 + [whole] * 3 + [pl.BlockSpec(memory_space=pl.ANY)],
        out_specs=[grid_line] * 5,
        scratch_shapes=[
            pltpu.VMEM((2, 2, 2, WAVES, STRIP), jnp.bfloat16),
            pltpu.VMEM((2, STRIPS * 40, WAVES), jnp.bfloat16),
            pltpu.VMEM((2, STRIPS * 40, WAVES), jnp.bfloat16),
            pltpu.VMEM((2, 8, WAVES), jnp.float32),
            pltpu.VMEM((6, 8, WAVES), jnp.float32),
            pltpu.VMEM((3, 4, 640), jnp.float32),
            pltpu.SemaphoreType.DMA((2,)),
        ],
        compiler_params=pltpu.CompilerParams(vmem_limit_bytes=50 * 2**20),
    )(lon_counts, lat_order, depth, diagonal, fourier, above, pair_row, basis)


def body(
    spectral, legendre, pair_list, lon_counts, lat_order, layer_depth_log, diagonal_layer_factor
):
    rows = jnp.transpose(spectral, (0, 2, 1, 3)).reshape(6, 648, 640)
    polynomials = jnp.transpose(legendre, (0, 2, 1))
    pair_row = pair_list.reshape(1, 640)
    row = jnp.arange(64)
    slots = (
        (row[:, None] % 2 == row[None, :] // 32)
        & (jnp.repeat(lat_order, 2)[:, None] == row[None, :] % 32)
    ).astype(jnp.bfloat16)
    fourier, above, basis = exchange(
        pair_list, lon_counts, lat_order, layer_depth_log, rows, polynomials, pair_row, slots
    )
    return tuple(
        synthesize(lon_counts, lat_order, layer_depth_log, diagonal_layer_factor, fourier,
                   above.reshape(16, 4, 128), pair_row, basis)
    )


def solution(mesh):
    placed = (
        P(None, "lev", "wave", None),
        P("wave", None, None),
        P(),
        P(),
        P(),
        P("lev"),
        P("lev"),
    )
    return jax.shard_map(
        body,
        mesh=mesh,
        in_specs=placed,
        out_specs=(P("wave", "lev", None),) * 5,
        check_vma=False,
    )
```

time: 286 us -> 120 us (0.42)
  waiting for transfers between devices: 142 us -> 0 us
  Pallas kernels: 34.3 us -> 114 us
  local copies, waits for them, and re-layouts: 47.2 us -> 3.93 us
  blocking collectives: 24.9 us -> 0 us
  starting transfers between devices: 16.4 us -> 0 us
  other arithmetic: 12 us -> 0.71 us
  matrix products: 7.31 us -> 0 us
    all_to_all x2 -> x0, waiting for transfers between devices: 142 us -> none  [the longest x1 134 us: body(): lax.all_to_all(spectral, 'wave', split_axis=3, concat_axis=2, tiled=True)]
    pallas_call x1 -> x2, Pallas kernels: 34.3 us -> 114 us  [the longest x1 99.6 us: exchange(): pl.pallas_call(exchange_kernel, out_shape=[jax.ShapeDtypeStruct((2, 512,...]
    all_to_all x5 -> x0, local copies, waits for them, and re-layouts: 31.4 us -> none  [the longest x2 29.2 us: body(): lax.all_to_all(spectral, 'wave', split_axis=3, concat_axis=2, tiled=True)]
    all_gather x1 -> x0, blocking collectives: 24.9 us -> none  [body(): pieces = lax.all_gather(scaled, 'lev')]
    all_to_all x2 -> x0, starting transfers between devices: 16.4 us -> none  [the longest x1 8.67 us: body(): lax.all_to_all(values, 'wave', split_axis=0, concat_axis=4, tiled=True)]
    unnamed x13 -> x14, local copies, waits for them, and re-layouts: 14.1 us -> 1.82 us
    select_n x2, other arithmetic: 8.89 us -> 0.01 us  [the longest x1 0.01 us: body(): row[:, None] % 2 == row[None, :] // 32]
    dot_general x1 -> x0, matrix products: 7.31 us -> none  [legendre_split(): jnp.einsum('hclrp,prq->qhclp', stacked, polynomials, preferred_element_ty...]
  transfers between devices with their start and end apart: 2 -> 0, of which waited for: 2 -> 0; matrix products, arithmetic and copies ran while one was open for 1% -> 0% of each run, Pallas kernels for 0% -> 0%
where the time goes in v2:
time: 120 us; the launch traced here: 119 us
  Pallas kernels  114 us (95%)
  local copies, waits for them, and re-layouts  3.93 us (3%)
    pallas_call x1, Pallas kernels, exchange(): pl.pallas_call(exchange_kernel, out_shape=[jax.ShapeDtypeStruct((2, 512,...  99.6 us
    pallas_call x1, Pallas kernels, synthesize(): pl.pallas_call(synthesis_kernel, grid=(2,), out_shape=[jax.ShapeDtypeStru...  14.5 us

profile of v2, /device:TPU:1, one launch (start us, length us, event | category | flops | bytes accessed | tf_op | source)
XLA Modules:
  0.0 119.5 jit_solution(3135371873780133023)
XLA Ops:
  0.6 0.0 copy-start.3
  0.6 0.0 copy-start.5
  0.7 0.0 copy-start.4
  0.7 0.0 copy-start.6
  0.7 1.3 %reshape.88.pair_row = s32[1,640]{1,0:T(1,128)} reshape(s32[640]{0:T(1024)} %pairs.1) | data formatting | bytes 5120 | tf_op jit(solution)/shard_map/reshape | solution.py:466
  2.0 0.0 copy-start.2
  2.0 0.7 broadcast_in_dim.2
  2.7 0.1 eq.35
  2.8 0.7 and_convert_fusion.slots
  3.5 99.6 %shard_map.110 = (f32[2,512,128]{2,1,0:T(8,128)}, f32[64,128]{1,0:T(8,128)}, bf16[2,2,2,1280,768]{4,3,2,1,0:T(8,128)(2,1)}) custom-call(s32[640]{0:T(1024)} %pairs.1, s32[32]{0:T(128)} %lon_counts.3, s32[32]{0:T(128)} %lat_order.3, f32[8]{0:T(128)} %depth.3, bf16[6,648,640]{2,1,0:T(8,128)(2,1)} %bitcast.6, bf16[40,32,1296]{2,1,0:T(8,128)(2,1)} %bitcast.7, ...), custom_call_target="tpu_custom_call" | custom-call | tf_op jit(solution)/shard_map/pallas_call | solution.py:285
  103.1 0.0 copy-done.3
  103.1 0.0 copy-done.5
  103.1 0.0 copy-done.4
  103.2 0.0 copy-done.6
  103.2 0.0 copy-done.2
  103.2 0.0 copy-start
  103.2 1.0 copy-done
  104.2 0.0 copy-start.1
  104.2 0.8 copy-done.1
  105.0 14.5 %shard_map.111 = (f32[2,8,5376]{2,1,0:T(8,128)}, f32[2,8,5376]{2,1,0:T(8,128)}, f32[2,8,5376]{2,1,0:T(8,128)}, f32[2,8,5376]{2,1,0:T(8,128)}, f32[2,8,5376]{2,1,0:T(8,128)}) custom-call(s32[32]{0:T(128)S(1)} %copy-done.4, s32[32]{0:T(128)S(1)} %copy-done.3, f32[8]{0:T(128)S(1)} %copy-done.5, f32[8]{0:T(128)S(1)} %copy-done.6, f32[2,512,128]{2,1,0:T(8,128)S(1)} %copy-done, ...), custom_call_target="tpu_custom_call" | custom-call | tf_op jit(solution)/shard_map/pallas_call | solution.py:442
  (2 shorter events, 0.0 us)
Async XLA Ops:
  0.6 102.5 %copy-start.3 = (s32[32]{0:T(128)S(1)}, s32[32]{0:T(128)}, u32[]{:S(2)}) copy-start(s32[32]{0:T(128)} %lat_order.3) | copy-start | bytes 388
  0.6 102.5 %copy-start.5 = (f32[8]{0:T(128)S(1)}, f32[8]{0:T(128)}, u32[]{:S(2)}) copy-start(f32[8]{0:T(128)} %depth.3) | copy-start | bytes 100
  0.7 102.5 %copy-start.4 = (s32[32]{0:T(128)S(1)}, s32[32]{0:T(128)}, u32[]{:S(2)}) copy-start(s32[32]{0:T(128)} %lon_counts.3) | copy-start | bytes 388
  0.7 102.5 %copy-start.6 = (f32[8]{0:T(128)S(1)}, f32[8]{0:T(128)}, u32[]{:S(2)}) copy-start(f32[8]{0:T(128)} %diagonal.1) | copy-start | bytes 100
  2.0 101.2 %copy-start.2 = (s32[1,640]{1,0:T(1,128)S(1)}, s32[1,640]{1,0:T(1,128)}, u32[]{:S(2)}) copy-start(s32[1,640]{1,0:T(1,128)} %reshape.88.pair_row) | copy-start | bytes 7684
  103.2 1.0 copy-start
  104.2 0.8 copy-start.1

commit v3 on v2

--- a/solution.py
+++ b/solution.py
@@ -44,10 +44,10 @@
     return high, (value - high.astype(jnp.float32)).astype(jnp.bfloat16)
 
 
-def exchange_kernel(pairs, lon_counts, lat_order, depth, spectral, legendre, pair_row, slots,
-                    out_fourier, out_above, out_basis,
+def exchange_kernel(pairs, lon_counts, lat_order, depth, spectral, legendre,
+                    out_fourier, pair_row, out_basis,
                     spec, legs, send_a, send_b, got_a, got_b, stage, rights, lefts, shuffle,
-                    summed, send_f, got_f, send_c, got_c, column, table,
+                    summed, slots, send_f, got_f, send_c, got_c, column, table,
                     in_sem, leg_sem, spec_send, spec_recv, spec_own, four_send, four_recv, four_own,
                     lev_send, lev_recv, table_sem):
     wave, lev = lax.axis_index("wave"), lax.axis_index("lev")
@@ -133,7 +133,26 @@
         return 0
 
     lax.fori_loop(0, SHARE, masked, 0)
-    column[...] = jnp.transpose(jnp.broadcast_to(pair_row[...].astype(jnp.float32), (128, 640)))
+    lane = lax.broadcasted_iota(jnp.int32, (8, 128), 1)
+    for tile in range(5):
+        def listed(step, values, tile=tile):
+            for place in range(8):
+                at = step * 8 + place
+                values = jnp.where(lane == at, pairs[tile * 128 + at], values)
+            return values
+
+        values = lax.fori_loop(0, 16, listed, jnp.zeros((8, 128), jnp.int32)).astype(jnp.float32)
+        pair_row[:, tile * 128 : tile * 128 + 128] = values
+        column[tile * 128 : tile * 128 + 128, :] = jnp.transpose(jnp.broadcast_to(values[:1], (128, 128)))
+    row = lax.broadcasted_iota(jnp.int32, (64, 64), 0)
+    spot = lax.broadcasted_iota(jnp.int32, (64, 64), 1)
+    wanted = jnp.zeros((64, 64), jnp.int32)
+    for number in range(32):
+        here = (row % 16 == number // 2) & (row // 32 == number % 2)
+        wanted = jnp.where(here, lat_order[number], wanted)
+    wanted = wanted + 32 * ((row // 16) % 2)
+    slots[...] = jnp.where(spot == wanted, 1.0, 0.0).astype(jnp.bfloat16)
+    send_f[...] = jnp.zeros_like(send_f)
 
     def table_copy(lat, block):
         slot = lax.rem(block, 2)
@@ -214,28 +233,35 @@
             return 0
 
         lax.fori_loop(0, 4, levels, 0)
+
+    def in_order(rest):
+        moved = jnp.zeros(rest.shape, jnp.float32)
+        for _ in range(3):
+            piece = rest.astype(jnp.bfloat16)
+            rest = rest - piece.astype(jnp.float32)
+            moved = moved + times(slots[...], piece)
+        return moved
+
+    def send_fourier(part):
         for duo in range(4):
-            rest = summed[duo]
-            moved = jnp.zeros((64, 256), jnp.float32)
-            for _ in range(3):
-                piece = rest.astype(jnp.bfloat16)
-                rest = rest - piece.astype(jnp.float32)
-                moved = moved + times(slots[...], piece)
-            send_f[part, pl.ds(2 * duo, 64, stride=8), :] = moved[:, :128]
-            send_f[part, pl.ds(2 * duo + 1, 64, stride=8), :] = moved[:, 128:]
+            moved = in_order(summed[duo])
+            for place in range(4):
+                for odd in (0, 1):
+                    send_f[part, pl.ds(8 * place + 2 * duo + odd, 16, stride=40), :] = (
+                        moved[16 * place : 16 * place + 16, 128 * odd : 128 * odd + 128])
         here = []
         for number, (x, y) in enumerate(ORDER):
             other = lax.rem(across + x, 4) * 4 + lax.rem(along + y, 4)
             copy = pltpu.make_async_remote_copy(
-                src_ref=send_f.at[part, pl.ds(pl.multiple_of(other * 32, 32), 32), :],
-                dst_ref=got_f.at[part, pl.ds(pl.multiple_of(wave * 32, 32), 32), :],
+                src_ref=send_f.at[part, pl.ds(pl.multiple_of(other * 40, 8), 40), :],
+                dst_ref=got_f.at[part, pl.ds(pl.multiple_of(wave * 40, 8), 40), :],
                 send_sem=four_send.at[part, number], recv_sem=four_recv.at[part, number],
                 device_id=(other, lev), device_id_type=MESH)
             copy.start()
             here.append(copy)
         own = pltpu.make_async_copy(
-            send_f.at[part, pl.ds(pl.multiple_of(wave * 32, 32), 32), :],
-            got_f.at[part, pl.ds(pl.multiple_of(wave * 32, 32), 32), :], four_own.at[part])
+            send_f.at[part, pl.ds(pl.multiple_of(wave * 40, 8), 40), :],
+            got_f.at[part, pl.ds(pl.multiple_of(wave * 40, 8), 40), :], four_own.at[part])
         own.start()
         copies.extend(here)
         return here, own
@@ -247,13 +273,11 @@
 
     tables(0)
     tables(1)
-    first = legendre_sums(1)
-    arrived(*first)
-    level = lax.broadcasted_iota(jnp.int32, (1, 8, 128), 1)
-    share = jnp.zeros((1, 8, 128), jnp.float32)
-    for number in range(8):
-        share = jnp.where(level == number, depth[number], share)
-    send_c[...] = jnp.sum(got_f[1].reshape(64, 8, 128) * share, axis=1)
+    legendre_sums(1)
+    lower = jnp.zeros((64, 128), jnp.float32)
+    for duo in range(4):
+        lower = lower + depth[2 * duo] * summed[duo, :, :128] + depth[2 * duo + 1] * summed[duo, :, 128:]
+    send_c[...] = lower
     lev_copies = []
     for step in range(1, PEERS):
         copy = pltpu.make_async_remote_copy(
@@ -262,22 +286,26 @@
             device_id=(wave, lax.rem(lev + step, PEERS)), device_id_type=MESH)
         copy.start()
         lev_copies.append(copy)
-    out_fourier[1] = got_f[1]
-    second = legendre_sums(0)
+    first = send_fourier(1)
+    legendre_sums(0)
     for copy in lev_copies:
         copy.wait_recv()
     above = jnp.zeros((64, 128), jnp.float32)
     got_c[lev] = send_c[...]
     for other in range(PEERS):
         above = above + jnp.where(other > lev, got_c[other], 0.0)
-    out_above[...] = above
+    above = in_order(above)
+    for place in range(4):
+        send_f[0, pl.ds(32 + place, 16, stride=40), :] = above[16 * place : 16 * place + 16]
+    second = send_fourier(0)
+    arrived(*first)
     arrived(*second)
-    out_fourier[0] = got_f[0]
+    out_fourier[...] = got_f[...]
     for copy in copies + lev_copies:
         copy.wait_send()
 
 
-def exchange(pairs, lon_counts, lat_order, depth, spectral, legendre, pair_row, slots):
+def exchange(pairs, lon_counts, lat_order, depth, spectral, legendre):
     anywhere = pl.BlockSpec(memory_space=pl.ANY)
     vector = pl.BlockSpec(memory_space=pltpu.VMEM)
     scalar = pl.BlockSpec(memory_space=pltpu.SMEM)
@@ -285,11 +313,11 @@
     return pl.pallas_call(
         exchange_kernel,
         out_shape=[
-            jax.ShapeDtypeStruct((2, 512, 128), jnp.float32),
-            jax.ShapeDtypeStruct((64, 128), jnp.float32),
+            jax.ShapeDtypeStruct((2, PEERS * 40, 128), jnp.float32),
+            jax.ShapeDtypeStruct((8, 640), jnp.float32),
             jax.ShapeDtypeStruct((2, 2, 2, WAVES, STRIP), jnp.bfloat16),
         ],
-        in_specs=[scalar] * 4 + [anywhere] * 2 + [vector] * 2,
+        in_specs=[scalar] * 4 + [anywhere] * 2,
         out_specs=[vector, vector, anywhere],
         scratch_shapes=[
             pltpu.VMEM((6, 648, 640), jnp.bfloat16),
@@ -303,8 +331,9 @@
             pltpu.VMEM((SHARE * 64, 1296), jnp.bfloat16),
             pltpu.VMEM((8, 3, 256, 256), jnp.bfloat16),
             pltpu.VMEM((4, 64, 256), jnp.float32),
-            pltpu.VMEM((2, 512, 128), jnp.float32),
-            pltpu.VMEM((2, 512, 128), jnp.float32),
+            pltpu.VMEM((64, 64), jnp.bfloat16),
+            pltpu.VMEM((2, PEERS * 40, 128), jnp.float32),
+            pltpu.VMEM((2, PEERS * 40, 128), jnp.float32),
             pltpu.VMEM((64, 128), jnp.float32),
             pltpu.VMEM((PEERS, 64, 128), jnp.float32),
             pltpu.VMEM((640, 128), jnp.float32),
@@ -315,12 +344,12 @@
         compiler_params=pltpu.CompilerParams(
             collective_id=0, has_side_effects=True, vmem_limit_bytes=56 * 2**20
         ),
-    )(pairs, lon_counts, lat_order, depth, spectral, legendre, pair_row, slots)
-
-
-def synthesis_kernel(lon_counts, lat_order, depth, diagonal, fourier, above, pair_row, basis,
+    )(pairs, lon_counts, lat_order, depth, spectral, legendre)
+
+
+def synthesis_kernel(lon_counts, lat_order, depth, diagonal, fourier_far, pair_far, basis,
                      out_v, out_d, out_t, out_s, out_h,
-                     table, left_high, left_low, twist, coef, upper, table_sem):
+                     table, left_high, left_low, twist, coef, upper, fourier, pair_row, table_sem):
     lat = pl.program_id(0)
     wave_group = lax.axis_index("wave")
 
@@ -329,8 +358,14 @@
 
     @pl.when(lat == 0)
     def _():
+        near = (pltpu.make_async_copy(pair_far, pair_row, table_sem.at[2]),
+                pltpu.make_async_copy(fourier_far, fourier, table_sem.at[3]))
+        for copy in near:
+            copy.start()
         load(0).start()
         load(1).start()
+        for copy in near:
+            copy.wait()
 
     circle_whole = lon_counts[lat_order[2 * wave_group + lat]]
     circle = jnp.full((1, 1), circle_whole, jnp.int32).astype(jnp.float32)
@@ -354,7 +389,7 @@
     for part in range(2):
         for side in range(2):
             def take(source, part=part, side=side):
-                return fourier[part, pl.ds(pl.multiple_of(source * 32 + lat * 16 + side * 8, 8), 8), :]
+                return fourier[part, pl.ds(pl.multiple_of(source * 40 + lat * 16 + side * 8, 8), 8), :]
 
             def keep(place, tile, value, part=part, side=side):
                 at = side * 640 + tile * 128
@@ -363,14 +398,14 @@
             spread(take, keep, 8)
 
     def take_above(source):
-        return above[source]
+        return fourier[0, source * 40 + 32 : source * 40 + 36, :]
 
     def keep_above(place, tile, value):
         upper[place, :, tile * 128 : tile * 128 + 128] = value
 
     spread(take_above, keep_above, 4)
 
-    pair = pair_row[...].astype(jnp.float32)
+    pair = pair_row[:1, :]
     wave = jnp.concatenate([pair, TRUNC - pair], axis=1)
     weight = jnp.where(2.0 * wave < circle, jnp.where(wave == 0.0, 1.0, 2.0), 0.0)
     start = (lax.broadcasted_iota(jnp.int32, (8, WAVES), 0) * STRIP).astype(jnp.float32)
@@ -435,15 +470,15 @@
     lax.fori_loop(0, STRIP // 256, block_of, 0)
 
 
-def synthesize(lon_counts, lat_order, depth, diagonal, fourier, above, pair_row, basis):
-    whole = pl.BlockSpec(memory_space=pltpu.VMEM)
+def synthesize(lon_counts, lat_order, depth, diagonal, fourier, pair_row, basis):
+    anywhere = pl.BlockSpec(memory_space=pl.ANY)
     scalar = pl.BlockSpec(memory_space=pltpu.SMEM)
     grid_line = pl.BlockSpec((1, 8, LON_PAD), lambda i: (i, 0, 0))
     return pl.pallas_call(
         synthesis_kernel,
         grid=(2,),
         out_shape=[jax.ShapeDtypeStruct((2, 8, LON_PAD), jnp.float32)] * 5,
-        in_specs=[scalar] * 4 + [whole] * 3 + [pl.BlockSpec(memory_space=pl.ANY)],
+        in_specs=[scalar] * 4 + [anywhere] * 3,
         out_specs=[grid_line] * 5,
         scratch_shapes=[
             pltpu.VMEM((2, 2, 2, WAVES, STRIP), jnp.bfloat16),
@@ -452,10 +487,12 @@
             pltpu.VMEM((2, 8, WAVES), jnp.float32),
             pltpu.VMEM((6, 8, WAVES), jnp.float32),
             pltpu.VMEM((3, 4, 640), jnp.float32),
-            pltpu.SemaphoreType.DMA((2,)),
+            pltpu.VMEM((2, PEERS * 40, 128), jnp.float32),
+            pltpu.VMEM((8, 640), jnp.float32),
+            pltpu.SemaphoreType.DMA((4,)),
         ],
-        compiler_params=pltpu.CompilerParams(vmem_limit_bytes=50 * 2**20),
-    )(lon_counts, lat_order, depth, diagonal, fourier, above, pair_row, basis)
+        compiler_params=pltpu.CompilerParams(vmem_limit_bytes=60 * 2**20),
+    )(lon_counts, lat_order, depth, diagonal, fourier, pair_row, basis)
 
 
 def body(
@@ -463,18 +500,11 @@
 ):
     rows = jnp.transpose(spectral, (0, 2, 1, 3)).reshape(6, 648, 640)
     polynomials = jnp.transpose(legendre, (0, 2, 1))
-    pair_row = pair_list.reshape(1, 640)
-    row = jnp.arange(64)
-    slots = (
-        (row[:, None] % 2 == row[None, :] // 32)
-        & (jnp.repeat(lat_order, 2)[:, None] == row[None, :] % 32)
-    ).astype(jnp.bfloat16)
-    fourier, above, basis = exchange(
-        pair_list, lon_counts, lat_order, layer_depth_log, rows, polynomials, pair_row, slots
+    fourier, pair_row, basis = exchange(
+        pair_list, lon_counts, lat_order, layer_depth_log, rows, polynomials
     )
     return tuple(
-        synthesize(lon_counts, lat_order, layer_depth_log, diagonal_layer_factor, fourier,
-                   above.reshape(16, 4, 128), pair_row, basis)
+        synthesize(lon_counts, lat_order, layer_depth_log, diagonal_layer_factor, fourier, pair_row, basis)
     )
 
 

time: 120 us -> 112 us (0.933)
  local copies, waits for them, and re-layouts: 3.93 us -> 0 us
  Pallas kernels: 114 us -> 112 us
    pallas_call x1, Pallas kernels: 99.6 us -> 97.4 us  [exchange(): pl.pallas_call(exchange_kernel, out_shape=[jax.ShapeDtypeStruct((2, PEERS...]
    unnamed x14 -> x0, local copies, waits for them, and re-layouts: 1.82 us -> none
    reshape x1 -> x0, local copies, waits for them, and re-layouts: 1.27 us -> none  [body(): pair_row = pair_list.reshape(1, 640)]
where the time goes in v3:
time: 112 us
  Pallas kernels  112 us (100%)
    pallas_call x1, Pallas kernels, exchange(): pl.pallas_call(exchange_kernel, out_shape=[jax.ShapeDtypeStruct((2, PEERS...  97.4 us
    pallas_call x1, Pallas kernels, synthesize(): pl.pallas_call(synthesis_kernel, grid=(2,), out_shape=[jax.ShapeDtypeStru...  14.2 us

profile of v3, /device:TPU:1, one launch (start us, length us, event | category | flops | bytes accessed | tf_op | source)
XLA Modules:
  0.0 112.2 jit_solution(12463154182360837387)
XLA Ops:
  0.6 97.4 %shard_map.110 = (f32[2,640,128]{2,1,0:T(8,128)}, f32[8,640]{1,0:T(8,128)}, bf16[2,2,2,1280,768]{4,3,2,1,0:T(8,128)(2,1)}) custom-call(s32[640]{0:T(1024)} %pairs.1, s32[32]{0:T(128)} %lon_counts.3, s32[32]{0:T(128)} %lat_order.3, f32[8]{0:T(128)} %depth.3, bf16[6,648,640]{2,1,0:T(8,128)(2,1)} %bitcast.4, bf16[40,32,1296]{2,1,0:T(8,128)(2,1)} %bitcast.5), custom_call_target="tpu_custom_call" | custom-call | tf_op jit(solution)/shard_map/pallas_call | solution.py:313
  98.0 14.2 %shard_map.111 = (f32[2,8,5376]{2,1,0:T(8,128)}, f32[2,8,5376]{2,1,0:T(8,128)}, f32[2,8,5376]{2,1,0:T(8,128)}, f32[2,8,5376]{2,1,0:T(8,128)}, f32[2,8,5376]{2,1,0:T(8,128)}) custom-call(s32[32]{0:T(128)} %lon_counts.3, s32[32]{0:T(128)} %lat_order.3, f32[8]{0:T(128)} %depth.3, f32[8]{0:T(128)} %diagonal.1, f32[2,640,128]{2,1,0:T(8,128)} %get-tuple-element.8.fourier_far, ...), custom_call_target="tpu_custom_call" | custom-call | tf_op jit(solution)/shard_map/pallas_call | solution.py:477

commit v4 on v3

--- a/solution.py
+++ b/solution.py
@@ -47,7 +47,7 @@
 def exchange_kernel(pairs, lon_counts, lat_order, depth, spectral, legendre,
                     out_fourier, pair_row, out_basis,
                     spec, legs, send_a, send_b, got_a, got_b, stage, rights, lefts, shuffle,
-                    summed, slots, send_f, got_f, send_c, got_c, column, table,
+                    summed, halved, slots, send_f, got_f, send_c, got_c, column, table,
                     in_sem, leg_sem, spec_send, spec_recv, spec_own, four_send, four_recv, four_own,
                     lev_send, lev_recv, table_sem):
     wave, lev = lax.axis_index("wave"), lax.axis_index("lev")
@@ -77,8 +77,10 @@
         lane = lax.broadcasted_iota(jnp.int32, (1, 256), 1)
         second = jnp.where(lane >= 128, 1, 0)
         inner = lane - 128 * second
-        third = jnp.where(inner >= 40, 1, 0) + jnp.where(inner >= 80, 1, 0) + jnp.where(inner >= 120, 1, 0)
-        source = 80 * duo - window(duo) + 40 * second + inner - 40 * third
+        side = jnp.where(inner >= 60, 1, 0)
+        inner = inner - 60 * side
+        third = jnp.where(inner >= 20, 1, 0) + jnp.where(inner >= 40, 1, 0) + jnp.where(inner >= 60, 1, 0)
+        source = 80 * duo - window(duo) + 40 * second + 20 * side + inner - 20 * third
         row = lax.broadcasted_iota(jnp.int32, (256, 256), 0)
         for place in range(3):
             wanted = jnp.where(third == place, source, -1)
@@ -210,29 +212,43 @@
 
         def gather(chunk, _):
             rows = pl.ds(pl.multiple_of(chunk * 144, 16), 144)
-            for level in range(8):
-                taken = stage[pl.ds(chunk * 1152 + level, 144, stride=8), :]
-                lanes = slice(128 * (level % 2), 128 * (level % 2) + 128)
-                rights[level // 2, rows, lanes] = taken.astype(jnp.bfloat16)
+            for duo in range(4):
+                even = stage[pl.ds(chunk * 1152 + 2 * duo, 144, stride=8), :]
+                odd = stage[pl.ds(chunk * 1152 + 2 * duo + 1, 144, stride=8), :]
+                lower = jnp.where(left_lane, even, pltpu.roll(odd, 64, 1))
+                upper = jnp.where(left_lane, pltpu.roll(even, 68, 1), pltpu.roll(odd, 4, 1))
+                lanes = slice(128 * (duo % 2), 128 * (duo % 2) + 128)
+                rights[duo // 2, rows, lanes] = lower.astype(jnp.bfloat16)
+                rights[2 + duo // 2, rows, lanes] = upper.astype(jnp.bfloat16)
             return 0
 
+        left_lane = lax.broadcasted_iota(jnp.int32, (1, 128), 1) < 64
         lax.fori_loop(0, 9, gather, 0)
-        lane = lax.broadcasted_iota(jnp.int32, (1, 256), 1)
-        inner = jnp.where(lane >= 128, lane - 128, lane)
-        inner = jnp.where(inner >= 80, inner - 80, jnp.where(inner >= 40, inner - 40, inner))
-
-        def levels(duo, _):
+        inner = lax.broadcasted_iota(jnp.int32, (1, 256), 1)
+        for step in (128, 64, 40, 20):
+            inner = jnp.where(inner >= step, inner - step, inner)
+
+        def levels(block, _):
+            side = block // 2
+
             def group(chunk, total):
-                result = times(lefts[pl.ds(pl.multiple_of(chunk * 512, 512), 512), :], rights[duo])
-                for place in range(8):
-                    total = total + jnp.where(inner == chunk * 8 + place,
+                first = pl.multiple_of(side * 1280 + chunk * 640, 128)
+                result = times(lefts[pl.ds(first, 640), :], rights[block])
+                for place in range(10):
+                    total = total + jnp.where(inner == chunk * 10 + place,
                                               result[place * 64 : place * 64 + 64], 0.0)
                 return total
 
-            summed[duo] = lax.fori_loop(0, 5, group, jnp.zeros((64, 256), jnp.float32))
+            total = lax.fori_loop(0, 2, group, jnp.zeros((64, 256), jnp.float32))
+            halved[block] = total
             return 0
 
         lax.fori_loop(0, 4, levels, 0)
+        for duo in range(4):
+            lanes = slice(128 * (duo % 2), 128 * (duo % 2) + 128)
+            lower, upper = halved[duo // 2, :, lanes], halved[2 + duo // 2, :, lanes]
+            summed[duo, :, :128] = jnp.where(left_lane, lower, pltpu.roll(upper, 64, 1))
+            summed[duo, :, 128:] = jnp.where(left_lane, pltpu.roll(lower, 64, 1), upper)
 
     def in_order(rest):
         moved = jnp.zeros(rest.shape, jnp.float32)
@@ -331,6 +347,7 @@
             pltpu.VMEM((SHARE * 64, 1296), jnp.bfloat16),
             pltpu.VMEM((8, 3, 256, 256), jnp.bfloat16),
             pltpu.VMEM((4, 64, 256), jnp.float32),
+            pltpu.VMEM((4, 64, 256), jnp.float32),
             pltpu.VMEM((64, 64), jnp.bfloat16),
             pltpu.VMEM((2, PEERS * 40, 128), jnp.float32),
             pltpu.VMEM((2, PEERS * 40, 128), jnp.float32),
@@ -349,7 +366,7 @@
 
 def synthesis_kernel(lon_counts, lat_order, depth, diagonal, fourier_far, pair_far, basis,
                      out_v, out_d, out_t, out_s, out_h,
-                     table, left_high, left_low, twist, coef, upper, fourier, pair_row, table_sem):
+                     table, left, twist, coef, upper, fourier, pair_row, table_sem):
     lat = pl.program_id(0)
     wave_group = lax.axis_index("wave")
 
@@ -368,7 +385,7 @@
             copy.wait()
 
     circle_whole = lon_counts[lat_order[2 * wave_group + lat]]
-    circle = jnp.full((1, 1), circle_whole, jnp.int32).astype(jnp.float32)
+    low_rows = STRIPS * 40
     lane = lax.broadcasted_iota(jnp.int32, (1, 128), 1)
 
     def spread(take, keep, height):
@@ -376,75 +393,85 @@
             tiles = [jnp.zeros((height, 128), jnp.float32)] * 5
             for source in range(PEERS):
                 value = take(source)
-                goal = source * SHARE
-                tile, offset = goal // 128, goal % 128
-                rolled = pltpu.roll(value, (offset - place * SHARE) % 128, 1)
-                end = offset + SHARE
-                tiles[tile] = jnp.where((lane >= offset) & (lane < end), rolled, tiles[tile])
-                if end > 128:
-                    tiles[tile + 1] = jnp.where(lane < end - 128, rolled, tiles[tile + 1])
+                for side in range(2):
+                    goal = source * SHARE + 20 * side
+                    tile, offset = goal // 128, goal % 128
+                    rolled = pltpu.roll(value, (offset - place * 20 - 64 * side) % 128, 1)
+                    end = offset + 20
+                    tiles[tile] = jnp.where((lane >= offset) & (lane < end), rolled, tiles[tile])
+                    if end > 128:
+                        tiles[tile + 1] = jnp.where(lane < end - 128, rolled, tiles[tile + 1])
             for tile in range(5):
                 keep(place, tile, tiles[tile])
 
-    for part in range(2):
-        for side in range(2):
-            def take(source, part=part, side=side):
-                return fourier[part, pl.ds(pl.multiple_of(source * 40 + lat * 16 + side * 8, 8), 8), :]
-
-            def keep(place, tile, value, part=part, side=side):
-                at = side * 640 + tile * 128
-                coef[3 * part + place, :, at : at + 128] = value
-
-            spread(take, keep, 8)
-
-    def take_above(source):
-        return fourier[0, source * 40 + 32 : source * 40 + 36, :]
-
-    def keep_above(place, tile, value):
-        upper[place, :, tile * 128 : tile * 128 + 128] = value
-
-    spread(take_above, keep_above, 4)
-
-    pair = pair_row[:1, :]
-    wave = jnp.concatenate([pair, TRUNC - pair], axis=1)
-    weight = jnp.where(2.0 * wave < circle, jnp.where(wave == 0.0, 1.0, 2.0), 0.0)
-    start = (lax.broadcasted_iota(jnp.int32, (8, WAVES), 0) * STRIP).astype(jnp.float32)
-    cosine, sine = turn(start * wave, circle)
-    twist[0] = cosine * weight
-    twist[1] = sine * weight
-    factor = wave * (1.0 / (TRUNC + 1))
-    level_of = lax.broadcasted_iota(jnp.int32, (8, 1), 0)
-
-    def rows_of(field):
-        if field < 3:
-            return coef[2 * field], coef[2 * field + 1]
-        real, imaginary = coef[4], coef[5]
-        if field == 3:
-            return -factor * imaginary, factor * real
-        higher = []
-        for value, place in ((real, 1), (imaginary, 2)):
-            total = jnp.broadcast_to(
-                jnp.concatenate([upper[place, pl.ds(2 * lat, 1), :], upper[place, pl.ds(2 * lat + 1, 1), :]], axis=1),
-                (8, WAVES))
-            for level in range(8):
-                share = jnp.where(level_of == level, diagonal[level],
-                                  jnp.where(level_of < level, depth[level], 0.0))
-                total = total + share * value[level : level + 1, :]
-            higher.append(total)
-        return higher[0], higher[1]
-
-    for field in range(5):
-        real, imaginary = rows_of(field)
-        for strip in range(STRIPS):
-            at = strip * 40 + field * 8
-            cosine = twist[0, strip : strip + 1, :]
-            sine = twist[1, strip : strip + 1, :]
-            high, low = halves(real * cosine - imaginary * sine)
-            left_high[0, at : at + 8, :] = high
-            left_low[0, at : at + 8, :] = low
-            high, low = halves(-(real * sine + imaginary * cosine))
-            left_high[1, at : at + 8, :] = high
-            left_low[1, at : at + 8, :] = low
+    def turned(which, _):
+        count = lon_counts[lat_order[2 * wave_group + which]]
+        circle = jnp.full((1, 1), count, jnp.int32).astype(jnp.float32)
+        for part in range(2):
+            for side in range(2):
+                def take(source, part=part, side=side):
+                    return fourier[part, pl.ds(pl.multiple_of(source * 40 + which * 16 + side * 8, 8), 8), :]
+
+                def keep(place, tile, value, part=part, side=side):
+                    at = side * 640 + tile * 128
+                    coef[3 * part + place, :, at : at + 128] = value
+
+                spread(take, keep, 8)
+
+        def take_above(source):
+            return fourier[0, source * 40 + 32 : source * 40 + 36, :]
+
+        def keep_above(place, tile, value):
+            upper[place, :, tile * 128 : tile * 128 + 128] = value
+
+        spread(take_above, keep_above, 4)
+
+        pair = pair_row[:1, :]
+        wave = jnp.concatenate([pair, TRUNC - pair], axis=1)
+        weight = jnp.where(2.0 * wave < circle, jnp.where(wave == 0.0, 1.0, 2.0), 0.0)
+        start = (lax.broadcasted_iota(jnp.int32, (8, WAVES), 0) * STRIP).astype(jnp.float32)
+        cosine, sine = turn(start * wave, circle)
+        twist[0] = cosine * weight
+        twist[1] = sine * weight
+        factor = wave * (1.0 / (TRUNC + 1))
+        level_of = lax.broadcasted_iota(jnp.int32, (8, 1), 0)
+
+        def rows_of(field):
+            if field < 3:
+                return coef[2 * field], coef[2 * field + 1]
+            real, imaginary = coef[4], coef[5]
+            if field == 3:
+                return -factor * imaginary, factor * real
+            higher = []
+            for value, place in ((real, 1), (imaginary, 2)):
+                total = jnp.broadcast_to(
+                    jnp.concatenate([upper[place, pl.ds(2 * which, 1), :], upper[place, pl.ds(2 * which + 1, 1), :]], axis=1),
+                    (8, WAVES))
+                for level in range(8):
+                    share = jnp.where(level_of == level, diagonal[level],
+                                      jnp.where(level_of < level, depth[level], 0.0))
+                    total = total + share * value[level : level + 1, :]
+                higher.append(total)
+            return higher[0], higher[1]
+
+        for field in range(5):
+            real, imaginary = rows_of(field)
+            for strip in range(STRIPS):
+                at = strip * 40 + field * 8
+                cosine = twist[0, strip : strip + 1, :]
+                sine = twist[1, strip : strip + 1, :]
+                high, low = halves(real * cosine - imaginary * sine)
+                left[which, 0, at : at + 8, :] = high
+                left[which, 0, low_rows + at : low_rows + at + 8, :] = low
+                high, low = halves(-(real * sine + imaginary * cosine))
+                left[which, 1, at : at + 8, :] = high
+                left[which, 1, low_rows + at : low_rows + at + 8, :] = low
+
+        return 0
+
+    @pl.when(lat == 0)
+    def _():
+        lax.fori_loop(0, 2, turned, 0)
 
     load(lat).wait()
 
@@ -455,8 +482,9 @@
         result = None
         for trig in (0, 1):
             high = table[lat, 0, trig, :, columns]
-            term = (times(left_high[trig], high) + times(left_low[trig], high)
-                    + times(left_high[trig], table[lat, 1, trig, :, columns]))
+            both = times(left[lat, trig], high)
+            term = (both[:low_rows] + both[low_rows:]
+                    + times(left[lat, trig, :low_rows], table[lat, 1, trig, :, columns]))
             result = term if result is None else result + term
         number = lax.broadcasted_iota(jnp.int32, (40, 256), 1) + first
         for strip in range(STRIPS):
@@ -482,8 +510,7 @@
         out_specs=[grid_line] * 5,
         scratch_shapes=[
             pltpu.VMEM((2, 2, 2, WAVES, STRIP), jnp.bfloat16),
-            pltpu.VMEM((2, STRIPS * 40, WAVES), jnp.bfloat16),
-            pltpu.VMEM((2, STRIPS * 40, WAVES), jnp.bfloat16),
+            pltpu.VMEM((2, 2, STRIPS * 80, WAVES), jnp.bfloat16),
             pltpu.VMEM((2, 8, WAVES), jnp.float32),
             pltpu.VMEM((6, 8, WAVES), jnp.float32),
             pltpu.VMEM((3, 4, 640), jnp.float32),

time: 112 us -> 106 us (0.946)
  Pallas kernels: 112 us -> 105 us
    pallas_call x1, Pallas kernels: 97.4 us -> 92.2 us  [exchange(): pl.pallas_call(exchange_kernel, out_shape=[jax.ShapeDtypeStruct((2, PEERS...]
where the time goes in v4:
time: 106 us
  Pallas kernels  105 us (99%)
    pallas_call x1, Pallas kernels, exchange(): pl.pallas_call(exchange_kernel, out_shape=[jax.ShapeDtypeStruct((2, PEERS...  92.2 us
    pallas_call x1, Pallas kernels, synthesize(): pl.pallas_call(synthesis_kernel, grid=(2,), out_shape=[jax.ShapeDtypeStru...  13.1 us

profile of v4, /device:TPU:1, one launch (start us, length us, event | category | flops | bytes accessed | tf_op | source)
XLA Modules:
  0.0 105.9 jit_solution(8799951342574636757)
XLA Ops:
  0.6 92.2 %shard_map.110 = (f32[2,640,128]{2,1,0:T(8,128)}, f32[8,640]{1,0:T(8,128)}, bf16[2,2,2,1280,768]{4,3,2,1,0:T(8,128)(2,1)}) custom-call(s32[640]{0:T(1024)} %pairs.1, s32[32]{0:T(128)} %lon_counts.3, s32[32]{0:T(128)} %lat_order.3, f32[8]{0:T(128)} %depth.3, bf16[6,648,640]{2,1,0:T(8,128)(2,1)} %bitcast.4, bf16[40,32,1296]{2,1,0:T(8,128)(2,1)} %bitcast.5), custom_call_target="tpu_custom_call" | custom-call | tf_op jit(solution)/shard_map/pallas_call | solution.py:329
  92.8 13.1 %shard_map.111 = (f32[2,8,5376]{2,1,0:T(8,128)}, f32[2,8,5376]{2,1,0:T(8,128)}, f32[2,8,5376]{2,1,0:T(8,128)}, f32[2,8,5376]{2,1,0:T(8,128)}, f32[2,8,5376]{2,1,0:T(8,128)}) custom-call(s32[32]{0:T(128)} %lon_counts.3, s32[32]{0:T(128)} %lat_order.3, f32[8]{0:T(128)} %depth.3, f32[8]{0:T(128)} %diagonal.1, f32[2,640,128]{2,1,0:T(8,128)} %get-tuple-element.8.fourier_far, ...), custom_call_target="tpu_custom_call" | custom-call | tf_op jit(solution)/shard_map/pallas_call | solution.py:505

commit v5 on v4

--- a/solution.py
+++ b/solution.py
@@ -45,9 +45,9 @@
 
 
 def exchange_kernel(pairs, lon_counts, lat_order, depth, spectral, legendre,
-                    out_fourier, pair_row, out_basis,
+                    out_fourier, pair_row, warm_t, warm_s, out_basis,
                     spec, legs, send_a, send_b, got_a, got_b, stage, rights, lefts, shuffle,
-                    summed, halved, slots, send_f, got_f, send_c, got_c, column, table,
+                    summed, halved, slots, send_f, got_f, send_c, got_c, column, table, coef, twist, left,
                     in_sem, leg_sem, spec_send, spec_recv, spec_own, four_send, four_recv, four_own,
                     lev_send, lev_recv, table_sem):
     wave, lev = lax.axis_index("wave"), lax.axis_index("lev")
@@ -73,22 +73,32 @@
     def window(duo):
         return jnp.minimum((80 * duo) // 128, 3) * 128
 
-    def shuffle_rows(duo, _):
-        lane = lax.broadcasted_iota(jnp.int32, (1, 256), 1)
-        second = jnp.where(lane >= 128, 1, 0)
-        inner = lane - 128 * second
-        side = jnp.where(inner >= 60, 1, 0)
-        inner = inner - 60 * side
+    def shuffle_rows(owner):
+        duo, second = owner // 2, lax.rem(owner, 2)
+        lane = lax.broadcasted_iota(jnp.int32, (1, 128), 1)
+        side = jnp.where(lane >= 60, 1, 0)
+        inner = lane - 60 * side
         third = jnp.where(inner >= 20, 1, 0) + jnp.where(inner >= 40, 1, 0) + jnp.where(inner >= 60, 1, 0)
         source = 80 * duo - window(duo) + 40 * second + 20 * side + inner - 20 * third
-        row = lax.broadcasted_iota(jnp.int32, (256, 256), 0)
+        row = lax.broadcasted_iota(jnp.int32, (256, 128), 0)
+        lanes = pl.ds(pl.multiple_of(second * 128, 128), 128)
         for place in range(3):
             wanted = jnp.where(third == place, source, -1)
-            shuffle[duo, place] = jnp.where(row == wanted, 1.0, 0.0).astype(jnp.bfloat16)
-        return 0
-
-    lax.fori_loop(0, 8, shuffle_rows, 0)
-    pl.semaphore_wait(barrier, 2 * (PEERS - 1))
+            shuffle[duo, place, :, lanes] = jnp.where(row == wanted, 1.0, 0.0).astype(jnp.bfloat16)
+
+    def shuffled_first(owner):
+        duo = owner // 2
+        lanes = pl.ds(pl.multiple_of(lax.rem(owner, 2) * 128, 128), 128)
+        source = pl.ds(pl.multiple_of(window(duo), 128), 256)
+        total = None
+        for place in range(3):
+            term = times(spec[3 + place, : HALVES[0], source], shuffle[duo, place, :, lanes])
+            total = term if total is None else total + term
+        send_a[1, owner] = total.astype(jnp.bfloat16)
+
+    def owner_of(x, y):
+        return lax.rem(across + x, 4) * 4 + lax.rem(along + y, 4)
+
 
     copies = []
     waits = {}
@@ -107,16 +117,26 @@
                 send[part, 2 * duo + 1] = total[:, 128:].astype(jnp.bfloat16)
                 return 0
 
-            lax.fori_loop(0, 8, shuffled, 0)
+            opening = part == 1 and half == 0
+            if not opening:
+                lax.fori_loop(0, 8, shuffled, 0)
             here = []
             for number, (x, y) in enumerate(ORDER):
-                other = lax.rem(across + x, 4) * 4 + lax.rem(along + y, 4)
+                other = owner_of(x, y)
+                if opening:
+                    shuffle_rows(other)
+                    shuffled_first(other)
+                    if number == 0:
+                        pl.semaphore_wait(barrier, 2 * (PEERS - 1))
                 copy = pltpu.make_async_remote_copy(
                     src_ref=send.at[part, other], dst_ref=got.at[part, wave],
                     send_sem=spec_send.at[part, half, number], recv_sem=spec_recv.at[part, half, number],
                     device_id=(other, lev), device_id_type=MESH)
                 copy.start()
                 here.append(copy)
+            if opening:
+                shuffle_rows(wave)
+                shuffled_first(wave)
             own = pltpu.make_async_copy(send.at[part, wave], got.at[part, wave], spec_own.at[part, half])
             own.start()
             waits[part, half] = (here, own)
@@ -156,45 +176,39 @@
     slots[...] = jnp.where(spot == wanted, 1.0, 0.0).astype(jnp.bfloat16)
     send_f[...] = jnp.zeros_like(send_f)
 
-    def table_copy(lat, block):
-        slot = lax.rem(block, 2)
-        return pltpu.make_async_copy(
-            table.at[slot], out_basis.at[lat, :, :, pl.ds(pl.multiple_of(block * 128, 128), 128), :],
-            table_sem.at[slot])
+    def circle_of(lat):
+        whole = lon_counts[lat_order[2 * wave + lat]]
+        return whole, jnp.full((1, 1), whole, jnp.int32).astype(jnp.float32)
+
+    def table_copy(lat):
+        return pltpu.make_async_copy(table.at[lat], out_basis.at[lat], table_sem.at[lat])
 
     def tables(lat):
-        whole = lon_counts[lat_order[2 * wave + lat]]
-        circle = jnp.full((1, 1), whole, jnp.int32).astype(jnp.float32)
-
-        def block_of(block, _):
-            slot = lax.rem(block, 2)
-
-            @pl.when(block >= 2)
-            def _():
-                table_copy(lat, block - 2).wait()
-
-            low = block < 5
-            at = (block - jnp.where(low, 0, 5)) * 128
-            base = jnp.where(low, 0.0, float(TRUNC))
-            sign = jnp.where(low, 1.0, -1.0)
-
-            def rows_of(step, _):
-                rows = pl.ds(pl.multiple_of(step * 16, 16), 16)
-                strip = lax.broadcasted_iota(jnp.int32, (16, STRIP), 1).astype(jnp.float32)
-                source = column[pl.ds(pl.multiple_of(at + step * 16, 16), 16), :]
-                number = jnp.concatenate([base + sign * source] * (STRIP // 128), axis=1)
-                cosine, sine = turn(number * strip, circle)
-                table[slot, 0, 0, rows, :], table[slot, 1, 0, rows, :] = halves(cosine)
-                table[slot, 0, 1, rows, :], table[slot, 1, 1, rows, :] = halves(sine)
-                return 0
-
-            lax.fori_loop(0, 8, rows_of, 0)
-            table_copy(lat, block).start()
+        _, circle = circle_of(lat)
+
+        def rows_of(step, _):
+            rows = pl.ds(pl.multiple_of(step * 16, 16), 16)
+            mirrored = pl.ds(pl.multiple_of(step * 16 + 640, 16), 16)
+            strip = lax.broadcasted_iota(jnp.int32, (16, STRIP), 1).astype(jnp.float32)
+            number = jnp.concatenate([column[rows, :]] * (STRIP // 128), axis=1)
+            for where, value in ((rows, number), (mirrored, TRUNC - number)):
+                cosine, sine = turn(value * strip, circle)
+                table[lat, 0, 0, where, :], table[lat, 1, 0, where, :] = halves(cosine)
+                table[lat, 0, 1, where, :], table[lat, 1, 1, where, :] = halves(sine)
             return 0
 
-        lax.fori_loop(0, 10, block_of, 0)
-        table_copy(lat, 8).wait()
-        table_copy(lat, 9).wait()
+        lax.fori_loop(0, 40, rows_of, 0)
+        table_copy(lat).start()
+
+    def twists(lat):
+        _, circle = circle_of(lat)
+        pair = pair_row[:1, :]
+        number = jnp.concatenate([pair, TRUNC - pair], axis=1)
+        weight = jnp.where(2.0 * number < circle, jnp.where(number == 0.0, 1.0, 2.0), 0.0)
+        start = (lax.broadcasted_iota(jnp.int32, (8, WAVES), 0) * STRIP).astype(jnp.float32)
+        cosine, sine = turn(start * number, circle)
+        twist[lat, 0] = cosine * weight
+        twist[lat, 1] = sine * weight
 
     def legendre_sums(part):
         for half in (0, 1):
@@ -287,8 +301,76 @@
             copy.wait_recv()
         own.wait()
 
-    tables(0)
-    tables(1)
+    line = lax.broadcasted_iota(jnp.int32, (1, 128), 1)
+
+    def spread(take, keep, height):
+        for place in range(3):
+            tiles = [jnp.zeros((height, 128), jnp.float32)] * 5
+            for source in range(PEERS):
+                value = take(source)
+                for side in range(2):
+                    goal = source * SHARE + 20 * side
+                    tile, offset = goal // 128, goal % 128
+                    rolled = pltpu.roll(value, (offset - place * 20 - 64 * side) % 128, 1)
+                    end = offset + 20
+                    tiles[tile] = jnp.where((line >= offset) & (line < end), rolled, tiles[tile])
+                    if end > 128:
+                        tiles[tile + 1] = jnp.where(line < end - 128, rolled, tiles[tile + 1])
+            for tile in range(5):
+                keep(place, tile, tiles[tile])
+
+    def warm(lat, _):
+        for side in range(2):
+            def take(source, side=side):
+                return got_f[1, pl.ds(pl.multiple_of(source * 40 + lat * 16 + side * 8, 8), 8), :]
+
+            def keep(place, tile, value, side=side):
+                at = side * 640 + tile * 128
+                coef[place, :, at : at + 128] = value
+
+            spread(take, keep, 8)
+        pair = pair_row[:1, :]
+        factor = jnp.concatenate([pair, TRUNC - pair], axis=1) * (1.0 / (TRUNC + 1))
+        low_rows = STRIPS * 16
+        for order in range(2):
+            real, imaginary = coef[1], coef[2]
+            if order == 1:
+                real, imaginary = -factor * imaginary, factor * real
+            for strip in range(STRIPS):
+                at = strip * 16 + order * 8
+                cosine = twist[lat, 0, strip : strip + 1, :]
+                sine = twist[lat, 1, strip : strip + 1, :]
+                high, low = halves(real * cosine - imaginary * sine)
+                left[0, at : at + 8, :] = high
+                left[0, low_rows + at : low_rows + at + 8, :] = low
+                high, low = halves(-(real * sine + imaginary * cosine))
+                left[1, at : at + 8, :] = high
+                left[1, low_rows + at : low_rows + at + 8, :] = low
+        whole, _ = circle_of(lat)
+
+        def block_of(block, _):
+            first = pl.multiple_of(block * 256, 256)
+            columns = pl.ds(first, 256)
+            result = None
+            for trig in (0, 1):
+                both = times(left[trig], table[lat, 0, trig, :, columns])
+                term = (both[:low_rows] + both[low_rows:]
+                        + times(left[trig, :low_rows], table[lat, 1, trig, :, columns]))
+                result = term if result is None else result + term
+            number = lax.broadcasted_iota(jnp.int32, (16, 256), 1) + first
+            for strip in range(STRIPS):
+                piece = jnp.where(number + strip * STRIP < whole, result[strip * 16 : strip * 16 + 16], 0.0)
+                where = pl.ds(pl.multiple_of(first + strip * STRIP, 256), 256)
+                warm_t[lat, :, where] = piece[:8]
+                warm_s[lat, :, where] = piece[8:]
+            return 0
+
+        lax.fori_loop(0, STRIP // 256, block_of, 0)
+        return 0
+
+    for lat in range(2):
+        twists(lat)
+        tables(lat)
     legendre_sums(1)
     lower = jnp.zeros((64, 128), jnp.float32)
     for duo in range(4):
@@ -315,10 +397,13 @@
         send_f[0, pl.ds(32 + place, 16, stride=40), :] = above[16 * place : 16 * place + 16]
     second = send_fourier(0)
     arrived(*first)
+    lax.fori_loop(0, 2, warm, 0)
     arrived(*second)
     out_fourier[...] = got_f[...]
     for copy in copies + lev_copies:
         copy.wait_send()
+    table_copy(0).wait()
+    table_copy(1).wait()
 
 
 def exchange(pairs, lon_counts, lat_order, depth, spectral, legendre):
@@ -331,10 +416,12 @@
         out_shape=[
             jax.ShapeDtypeStruct((2, PEERS * 40, 128), jnp.float32),
             jax.ShapeDtypeStruct((8, 640), jnp.float32),
+            jax.ShapeDtypeStruct((2, 8, LON_PAD), jnp.float32),
+            jax.ShapeDtypeStruct((2, 8, LON_PAD), jnp.float32),
             jax.ShapeDtypeStruct((2, 2, 2, WAVES, STRIP), jnp.bfloat16),
         ],
         in_specs=[scalar] * 4 + [anywhere] * 2,
-        out_specs=[vector, vector, anywhere],
+        out_specs=[vector] * 4 + [anywhere],
         scratch_shapes=[
             pltpu.VMEM((6, 648, 640), jnp.bfloat16),
             pltpu.VMEM((SHARE, 32, 1296), jnp.bfloat16),
@@ -354,17 +441,20 @@
             pltpu.VMEM((64, 128), jnp.float32),
             pltpu.VMEM((PEERS, 64, 128), jnp.float32),
             pltpu.VMEM((640, 128), jnp.float32),
-            pltpu.VMEM((2, 2, 2, 128, STRIP), jnp.bfloat16),
+            pltpu.VMEM((2, 2, 2, WAVES, STRIP), jnp.bfloat16),
+            pltpu.VMEM((3, 8, WAVES), jnp.float32),
+            pltpu.VMEM((2, 2, 8, WAVES), jnp.float32),
+            pltpu.VMEM((2, STRIPS * 32, WAVES), jnp.bfloat16),
             dma((2,)), dma, dma((2, 2, 15)), dma((2, 2, 15)), dma((2, 2)),
             dma((2, 15)), dma((2, 15)), dma((2,)), dma((15,)), dma((15,)), dma((2,)),
         ],
         compiler_params=pltpu.CompilerParams(
-            collective_id=0, has_side_effects=True, vmem_limit_bytes=56 * 2**20
+            collective_id=0, has_side_effects=True, vmem_limit_bytes=60 * 2**20
         ),
     )(pairs, lon_counts, lat_order, depth, spectral, legendre)
 
 
-def synthesis_kernel(lon_counts, lat_order, depth, diagonal, fourier_far, pair_far, basis,
+def synthesis_kernel(lon_counts, lat_order, depth, diagonal, fourier_far, pair_far, warm_t, warm_s, basis,
                      out_v, out_d, out_t, out_s, out_h,
                      table, left, twist, coef, upper, fourier, pair_row, table_sem):
     lat = pl.program_id(0)
@@ -372,6 +462,9 @@
 
     def load(which):
         return pltpu.make_async_copy(basis.at[which], table.at[which], table_sem.at[which])
+
+    passed = (pltpu.make_async_copy(warm_t, out_t, table_sem.at[4]),
+              pltpu.make_async_copy(warm_s, out_s, table_sem.at[5]))
 
     @pl.when(lat == 0)
     def _():
@@ -381,11 +474,13 @@
             copy.start()
         load(0).start()
         load(1).start()
+        for copy in passed:
+            copy.start()
         for copy in near:
             copy.wait()
 
     circle_whole = lon_counts[lat_order[2 * wave_group + lat]]
-    low_rows = STRIPS * 40
+    low_rows = STRIPS * 24
     lane = lax.broadcasted_iota(jnp.int32, (1, 128), 1)
 
     def spread(take, keep, height):
@@ -433,15 +528,12 @@
         cosine, sine = turn(start * wave, circle)
         twist[0] = cosine * weight
         twist[1] = sine * weight
-        factor = wave * (1.0 / (TRUNC + 1))
         level_of = lax.broadcasted_iota(jnp.int32, (8, 1), 0)
 
         def rows_of(field):
-            if field < 3:
+            if field < 2:
                 return coef[2 * field], coef[2 * field + 1]
             real, imaginary = coef[4], coef[5]
-            if field == 3:
-                return -factor * imaginary, factor * real
             higher = []
             for value, place in ((real, 1), (imaginary, 2)):
                 total = jnp.broadcast_to(
@@ -454,10 +546,10 @@
                 higher.append(total)
             return higher[0], higher[1]
 
-        for field in range(5):
+        for field in range(3):
             real, imaginary = rows_of(field)
             for strip in range(STRIPS):
-                at = strip * 40 + field * 8
+                at = strip * 24 + field * 8
                 cosine = twist[0, strip : strip + 1, :]
                 sine = twist[1, strip : strip + 1, :]
                 high, low = halves(real * cosine - imaginary * sine)
@@ -486,19 +578,24 @@
             term = (both[:low_rows] + both[low_rows:]
                     + times(left[lat, trig, :low_rows], table[lat, 1, trig, :, columns]))
             result = term if result is None else result + term
-        number = lax.broadcasted_iota(jnp.int32, (40, 256), 1) + first
+        number = lax.broadcasted_iota(jnp.int32, (24, 256), 1) + first
         for strip in range(STRIPS):
             piece = jnp.where(number + strip * STRIP < circle_whole,
-                              result[strip * 40 : strip * 40 + 40], 0.0)
+                              result[strip * 24 : strip * 24 + 24], 0.0)
             where = pl.ds(pl.multiple_of(first + strip * STRIP, 256), 256)
-            for field, out in enumerate((out_v, out_d, out_t, out_s, out_h)):
+            for field, out in enumerate((out_v, out_d, out_h)):
                 out[0, :, where] = piece[field * 8 : field * 8 + 8]
         return 0
 
     lax.fori_loop(0, STRIP // 256, block_of, 0)
 
-
-def synthesize(lon_counts, lat_order, depth, diagonal, fourier, pair_row, basis):
+    @pl.when(lat == 1)
+    def _():
+        for copy in passed:
+            copy.wait()
+
+
+def synthesize(lon_counts, lat_order, depth, diagonal, fourier, pair_row, warm_t, warm_s, basis):
     anywhere = pl.BlockSpec(memory_space=pl.ANY)
     scalar = pl.BlockSpec(memory_space=pltpu.SMEM)
     grid_line = pl.BlockSpec((1, 8, LON_PAD), lambda i: (i, 0, 0))
@@ -506,20 +603,20 @@
         synthesis_kernel,
         grid=(2,),
         out_shape=[jax.ShapeDtypeStruct((2, 8, LON_PAD), jnp.float32)] * 5,
-        in_specs=[scalar] * 4 + [anywhere] * 3,
-        out_specs=[grid_line] * 5,
+        in_specs=[scalar] * 4 + [anywhere] * 5,
+        out_specs=[grid_line, grid_line, anywhere, anywhere, grid_line],
         scratch_shapes=[
             pltpu.VMEM((2, 2, 2, WAVES, STRIP), jnp.bfloat16),
-            pltpu.VMEM((2, 2, STRIPS * 80, WAVES), jnp.bfloat16),
+            pltpu.VMEM((2, 2, STRIPS * 48, WAVES), jnp.bfloat16),
             pltpu.VMEM((2, 8, WAVES), jnp.float32),
             pltpu.VMEM((6, 8, WAVES), jnp.float32),
             pltpu.VMEM((3, 4, 640), jnp.float32),
             pltpu.VMEM((2, PEERS * 40, 128), jnp.float32),
             pltpu.VMEM((8, 640), jnp.float32),
-            pltpu.SemaphoreType.DMA((4,)),
+            pltpu.SemaphoreType.DMA((6,)),
         ],
         compiler_params=pltpu.CompilerParams(vmem_limit_bytes=60 * 2**20),
-    )(lon_counts, lat_order, depth, diagonal, fourier, pair_row, basis)
+    )(lon_counts, lat_order, depth, diagonal, fourier, pair_row, warm_t, warm_s, basis)
 
 
 def body(
@@ -527,11 +624,12 @@
 ):
     rows = jnp.transpose(spectral, (0, 2, 1, 3)).reshape(6, 648, 640)
     polynomials = jnp.transpose(legendre, (0, 2, 1))
-    fourier, pair_row, basis = exchange(
+    fourier, pair_row, warm_t, warm_s, basis = exchange(
         pair_list, lon_counts, lat_order, layer_depth_log, rows, polynomials
     )
     return tuple(
-        synthesize(lon_counts, lat_order, layer_depth_log, diagonal_layer_factor, fourier, pair_row, basis)
+        synthesize(lon_counts, lat_order, layer_depth_log, diagonal_layer_factor, fourier, pair_row,
+                   warm_t, warm_s, basis)
     )
 
 

time: 106 us -> 116 us (1.094)
  Pallas kernels: 105 us -> 115 us
    pallas_call x1, Pallas kernels: 13.1 us -> 23.5 us  [synthesize(): pl.pallas_call(synthesis_kernel, grid=(2,), out_shape=[jax.ShapeDtypeStru...]
where the time goes in v5:
time: 116 us; the launch traced here: 115 us
  Pallas kernels  115 us (99%)
    pallas_call x1, Pallas kernels, exchange(): pl.pallas_call(exchange_kernel, out_shape=[jax.ShapeDtypeStruct((2, PEERS...  91.3 us
    pallas_call x1, Pallas kernels, synthesize(): pl.pallas_call(synthesis_kernel, grid=(2,), out_shape=[jax.ShapeDtypeStru...  23.5 us

profile of v5, /device:TPU:1, one launch (start us, length us, event | category | flops | bytes accessed | tf_op | source)
XLA Modules:
  0.0 115.5 jit_solution(15546322928700665647)
XLA Ops:
  0.6 91.3 %shard_map.110 = (f32[2,640,128]{2,1,0:T(8,128)}, f32[8,640]{1,0:T(8,128)}, f32[2,8,5376]{2,1,0:T(8,128)}, f32[2,8,5376]{2,1,0:T(8,128)}, bf16[2,2,2,1280,768]{4,3,2,1,0:T(8,128)(2,1)}) custom-call(s32[640]{0:T(1024)} %pairs.1, s32[32]{0:T(128)} %lon_counts.3, s32[32]{0:T(128)} %lat_order.3, f32[8]{0:T(128)} %depth.3, bf16[6,648,640]{2,1,0:T(8,128)(2,1)} %bitcast.4, ...), custom_call_target="tpu_custom_call" | custom-call | tf_op jit(solution)/shard_map/pallas_call | solution.py:414
  91.9 23.5 %shard_map.111 = (f32[2,8,5376]{2,1,0:T(8,128)}, f32[2,8,5376]{2,1,0:T(8,128)}, f32[2,8,5376]{2,1,0:T(8,128)}, f32[2,8,5376]{2,1,0:T(8,128)}, f32[2,8,5376]{2,1,0:T(8,128)}) custom-call(s32[32]{0:T(128)} %lon_counts.3, s32[32]{0:T(128)} %lat_order.3, f32[8]{0:T(128)} %depth.3, f32[8]{0:T(128)} %diagonal.1, f32[2,640,128]{2,1,0:T(8,128)} %get-tuple-element.10.fourier_far, ...), custom_call_target="tpu_custom_call" | custom-call | tf_op jit(solution)/shard_map/pallas_call | solution.py:602

commit v6 on v5

--- a/solution.py
+++ b/solution.py
@@ -456,15 +456,15 @@
 
 def synthesis_kernel(lon_counts, lat_order, depth, diagonal, fourier_far, pair_far, warm_t, warm_s, basis,
                      out_v, out_d, out_t, out_s, out_h,
-                     table, left, twist, coef, upper, fourier, pair_row, table_sem):
+                     table, left, twist, coef, upper, fourier, pair_row, near_t, near_s, table_sem):
     lat = pl.program_id(0)
     wave_group = lax.axis_index("wave")
 
     def load(which):
         return pltpu.make_async_copy(basis.at[which], table.at[which], table_sem.at[which])
 
-    passed = (pltpu.make_async_copy(warm_t, out_t, table_sem.at[4]),
-              pltpu.make_async_copy(warm_s, out_s, table_sem.at[5]))
+    passed = (pltpu.make_async_copy(warm_t, near_t, table_sem.at[4]),
+              pltpu.make_async_copy(warm_s, near_s, table_sem.at[5]))
 
     @pl.when(lat == 0)
     def _():
@@ -589,10 +589,13 @@
 
     lax.fori_loop(0, STRIP // 256, block_of, 0)
 
-    @pl.when(lat == 1)
+    @pl.when(lat == 0)
     def _():
         for copy in passed:
             copy.wait()
+
+    out_t[0] = near_t[lat]
+    out_s[0] = near_s[lat]
 
 
 def synthesize(lon_counts, lat_order, depth, diagonal, fourier, pair_row, warm_t, warm_s, basis):
@@ -604,7 +607,7 @@
         grid=(2,),
         out_shape=[jax.ShapeDtypeStruct((2, 8, LON_PAD), jnp.float32)] * 5,
         in_specs=[scalar] * 4 + [anywhere] * 5,
-        out_specs=[grid_line, grid_line, anywhere, anywhere, grid_line],
+        out_specs=[grid_line] * 5,
         scratch_shapes=[
             pltpu.VMEM((2, 2, 2, WAVES, STRIP), jnp.bfloat16),
             pltpu.VMEM((2, 2, STRIPS * 48, WAVES), jnp.bfloat16),
@@ -613,6 +616,8 @@
             pltpu.VMEM((3, 4, 640), jnp.float32),
             pltpu.VMEM((2, PEERS * 40, 128), jnp.float32),
             pltpu.VMEM((8, 640), jnp.float32),
+            pltpu.VMEM((2, 8, LON_PAD), jnp.float32),
+            pltpu.VMEM((2, 8, LON_PAD), jnp.float32),
             pltpu.SemaphoreType.DMA((6,)),
         ],
         compiler_params=pltpu.CompilerParams(vmem_limit_bytes=60 * 2**20),

time: 116 us -> 103 us (0.89)
  Pallas kernels: 115 us -> 102 us
    pallas_call x1, Pallas kernels: 23.5 us -> 10.5 us  [synthesize(): pl.pallas_call(synthesis_kernel, grid=(2,), out_shape=[jax.ShapeDtypeStru...]
where the time goes in v6:
time: 103 us; the launch traced here: 102 us
  Pallas kernels  102 us (99%)
    pallas_call x1, Pallas kernels, exchange(): pl.pallas_call(exchange_kernel, out_shape=[jax.ShapeDtypeStruct((2, PEERS...  91.3 us
    pallas_call x1, Pallas kernels, synthesize(): pl.pallas_call(synthesis_kernel, grid=(2,), out_shape=[jax.ShapeDtypeStru...  10.5 us

profile of v6, /device:TPU:1, one launch (start us, length us, event | category | flops | bytes accessed | tf_op | source)
XLA Modules:
  0.0 102.4 jit_solution(4032640027286864457)
XLA Ops:
  0.6 91.3 %shard_map.110 = (f32[2,640,128]{2,1,0:T(8,128)}, f32[8,640]{1,0:T(8,128)}, f32[2,8,5376]{2,1,0:T(8,128)}, f32[2,8,5376]{2,1,0:T(8,128)}, bf16[2,2,2,1280,768]{4,3,2,1,0:T(8,128)(2,1)}) custom-call(s32[640]{0:T(1024)} %pairs.1, s32[32]{0:T(128)} %lon_counts.3, s32[32]{0:T(128)} %lat_order.3, f32[8]{0:T(128)} %depth.3, bf16[6,648,640]{2,1,0:T(8,128)(2,1)} %bitcast.4, ...), custom_call_target="tpu_custom_call" | custom-call | tf_op jit(solution)/shard_map/pallas_call | solution.py:414
  91.9 10.5 %shard_map.111 = (f32[2,8,5376]{2,1,0:T(8,128)}, f32[2,8,5376]{2,1,0:T(8,128)}, f32[2,8,5376]{2,1,0:T(8,128)}, f32[2,8,5376]{2,1,0:T(8,128)}, f32[2,8,5376]{2,1,0:T(8,128)}) custom-call(s32[32]{0:T(128)} %lon_counts.3, s32[32]{0:T(128)} %lat_order.3, f32[8]{0:T(128)} %depth.3, f32[8]{0:T(128)} %diagonal.1, f32[2,640,128]{2,1,0:T(8,128)} %get-tuple-element.10.fourier_far, ...), custom_call_target="tpu_custom_call" | custom-call | tf_op jit(solution)/shard_map/pallas_call | solution.py:605

commit v7 on v6

--- a/solution.py
+++ b/solution.py
@@ -15,7 +15,7 @@
 STRIPS = LON_PAD // STRIP
 PEERS = 16
 SHARE = 40
-HALVES = (320, 328)
+THIRDS = (208, 208, 232)
 ORDER = ((2, 2), (1, 0), (3, 0), (0, 1), (0, 3), (1, 2), (3, 2), (2, 1), (2, 3), (2, 0), (0, 2),
          (1, 1), (3, 3), (1, 3), (3, 1))
 MESH = pl.DeviceIdType.MESH
@@ -46,7 +46,7 @@
 
 def exchange_kernel(pairs, lon_counts, lat_order, depth, spectral, legendre,
                     out_fourier, pair_row, warm_t, warm_s, out_basis,
-                    spec, legs, send_a, send_b, got_a, got_b, stage, rights, lefts, shuffle,
+                    spec, legs, send_a, send_b, send_c3, got_a, got_b, got_c3, stage, rights, lefts, shuffle,
                     summed, halved, slots, send_f, got_f, send_c, got_c, column, table, coef, twist, left,
                     in_sem, leg_sem, spec_send, spec_recv, spec_own, four_send, four_recv, four_own,
                     lev_send, lev_recv, table_sem):
@@ -92,7 +92,7 @@
         source = pl.ds(pl.multiple_of(window(duo), 128), 256)
         total = None
         for place in range(3):
-            term = times(spec[3 + place, : HALVES[0], source], shuffle[duo, place, :, lanes])
+            term = times(spec[3 + place, : THIRDS[0], source], shuffle[duo, place, :, lanes])
             total = term if total is None else total + term
         send_a[1, owner] = total.astype(jnp.bfloat16)
 
@@ -104,8 +104,8 @@
     waits = {}
     for part in (1, 0):
         loads[1 - part].wait()
-        for half, (rows, send, got) in enumerate(zip(HALVES, (send_a, send_b), (got_a, got_b))):
-            first = half * HALVES[0]
+        for half, (rows, send, got) in enumerate(zip(THIRDS, (send_a, send_b, send_c3), (got_a, got_b, got_c3))):
+            first = half * THIRDS[0]
 
             def shuffled(duo, _, part=part, first=first, rows=rows, send=send):
                 lanes = pl.ds(pl.multiple_of(window(duo), 128), 256)
@@ -211,18 +211,17 @@
         twist[lat, 1] = sine * weight
 
     def legendre_sums(part):
-        for half in (0, 1):
+        for half, (rows, got) in enumerate(zip(THIRDS, (got_a, got_b, got_c3))):
             here, own = waits[part, half]
             for copy in here:
                 copy.wait_recv()
             own.wait()
 
-        def widen(source, _):
-            stage[pl.ds(pl.multiple_of(source * 648, 8), 320), :] = got_a[part, source].astype(jnp.float32)
-            stage[pl.ds(pl.multiple_of(source * 648 + 320, 8), 328), :] = got_b[part, source].astype(jnp.float32)
-            return 0
-
-        lax.fori_loop(0, PEERS, widen, 0)
+            def widen(source, _, rows=rows, got=got, first=half * THIRDS[0]):
+                stage[pl.ds(pl.multiple_of(source * 648 + first, 8), rows), :] = got[part, source].astype(jnp.float32)
+                return 0
+
+            lax.fori_loop(0, PEERS, widen, 0)
 
         def gather(chunk, _):
             rows = pl.ds(pl.multiple_of(chunk * 144, 16), 144)
@@ -425,10 +424,8 @@
         scratch_shapes=[
             pltpu.VMEM((6, 648, 640), jnp.bfloat16),
             pltpu.VMEM((SHARE, 32, 1296), jnp.bfloat16),
-            pltpu.VMEM((2, PEERS, HALVES[0], 128), jnp.bfloat16),
-            pltpu.VMEM((2, PEERS, HALVES[1], 128), jnp.bfloat16),
-            pltpu.VMEM((2, PEERS, HALVES[0], 128), jnp.bfloat16),
-            pltpu.VMEM((2, PEERS, HALVES[1], 128), jnp.bfloat16),
+            *[pltpu.VMEM((2, PEERS, rows, 128), jnp.bfloat16) for rows in THIRDS],
+            *[pltpu.VMEM((2, PEERS, rows, 128), jnp.bfloat16) for rows in THIRDS],
             pltpu.VMEM((PEERS * 648, 128), jnp.float32),
             pltpu.VMEM((4, 1296, 256), jnp.bfloat16),
             pltpu.VMEM((SHARE * 64, 1296), jnp.bfloat16),
@@ -445,7 +442,7 @@
             pltpu.VMEM((3, 8, WAVES), jnp.float32),
             pltpu.VMEM((2, 2, 8, WAVES), jnp.float32),
             pltpu.VMEM((2, STRIPS * 32, WAVES), jnp.bfloat16),
-            dma((2,)), dma, dma((2, 2, 15)), dma((2, 2, 15)), dma((2, 2)),
+            dma((2,)), dma, dma((2, 3, 15)), dma((2, 3, 15)), dma((2, 3)),
             dma((2, 15)), dma((2, 15)), dma((2,)), dma((15,)), dma((15,)), dma((2,)),
         ],
         compiler_params=pltpu.CompilerParams(

time: 103 us -> 102 us (level)
  no operation moved by 1% of the time
where the time goes in v7:
time: 102 us
  Pallas kernels  101 us (99%)
    pallas_call x1, Pallas kernels, exchange(): pl.pallas_call(exchange_kernel, out_shape=[jax.ShapeDtypeStruct((2, PEERS...  90.6 us
    pallas_call x1, Pallas kernels, synthesize(): pl.pallas_call(synthesis_kernel, grid=(2,), out_shape=[jax.ShapeDtypeStru...  10.5 us

profile of v7, /device:TPU:1, one launch (start us, length us, event | category | flops | bytes accessed | tf_op | source)
XLA Modules:
  0.0 101.7 jit_solution(6164180126065693644)
XLA Ops:
  0.6 90.6 %shard_map.110 = (f32[2,640,128]{2,1,0:T(8,128)}, f32[8,640]{1,0:T(8,128)}, f32[2,8,5376]{2,1,0:T(8,128)}, f32[2,8,5376]{2,1,0:T(8,128)}, bf16[2,2,2,1280,768]{4,3,2,1,0:T(8,128)(2,1)}) custom-call(s32[640]{0:T(1024)} %pairs.1, s32[32]{0:T(128)} %lon_counts.3, s32[32]{0:T(128)} %lat_order.3, f32[8]{0:T(128)} %depth.3, bf16[6,648,640]{2,1,0:T(8,128)(2,1)} %bitcast.4, ...), custom_call_target="tpu_custom_call" | custom-call | tf_op jit(solution)/shard_map/pallas_call | solution.py:413
  91.2 10.5 %shard_map.111 = (f32[2,8,5376]{2,1,0:T(8,128)}, f32[2,8,5376]{2,1,0:T(8,128)}, f32[2,8,5376]{2,1,0:T(8,128)}, f32[2,8,5376]{2,1,0:T(8,128)}, f32[2,8,5376]{2,1,0:T(8,128)}) custom-call(s32[32]{0:T(128)} %lon_counts.3, s32[32]{0:T(128)} %lat_order.3, f32[8]{0:T(128)} %depth.3, f32[8]{0:T(128)} %diagonal.1, f32[2,640,128]{2,1,0:T(8,128)} %get-tuple-element.10.fourier_far, ...), custom_call_target="tpu_custom_call" | custom-call | tf_op jit(solution)/shard_map/pallas_call | solution.py:602
